TPU v7x, 32 devices: a whole 2x2x4 slice. The times are simulated.
32 devices in a mesh: rows: 8 (over z, x), vecs: 4 (over y, core).
Axes of the slice: x: 2, y: 2, z: 4, core: 2. Of those that a mesh axis runs over, the one named last changes fastest.
Arguments:
- hamiltonian: float32 [256, 6, 128, 128], P('rows'), may hold values from -0.10825317 to 0.10825317
- columns: int32 [256, 6], P('rows'), may hold values from 0 to 255, as said below
- vectors: float32 [32768, 1024], P('rows', 'vecs'), may hold values from -6 to 6
- coefficients: float32 [7], replicated, may hold values from -1 to 1
Outputs:
- filtered: float32 [32768, 1024], P('rows', 'vecs')
- gram: float32 [1024, 1024], P('vecs', 'rows')
Inputs may be any that keep to these rules, and one draw needn't show every extreme that they name: The blocks of a block row have distinct columns; block row r has blocks in columns (r - 4) mod 256 and (r + 4) mod 256, and all its others within distance 4 - 1 of r, taken modulo 256.
All inputs are finite; a program needn't handle non-finite values.
Results may differ from a plain program's by a relative error of at most 0.0001.
Values sent between devices are 32-bit elements; how exact they have to be, the bound alone decides.
No kernel may reach another device: no remote copies, remote signals or barrier semaphores. Data moves between devices by JAX's collectives and lax.ppermute only.
A program may use at most 128 MiB of HBM per device.

v0:
```python
import jax
import jax.numpy as jnp
from jax import lax
from jax.sharding import PartitionSpec as P

BLOCK = 128
REACH = 4
ORDER = 6


def extended(shard, sides, width):
    for axis, dim in sides:
        peers, length = (lax.axis_size(axis), shard.shape[dim])
        up = [(i, (i + 1) % peers) for i in range(peers)]
        down = [(j, i) for i, j in up]
        last = lax.slice_in_dim(shard, length - width, length, axis=dim)
        initial = lax.slice_in_dim(shard, 0, width, axis=dim)
        before = lax.ppermute(last, axis, up)
        after = lax.ppermute(initial, axis, down)
        shard = jnp.concatenate([before, shard, after], axis=dim)
    return shard


def apply_operator(vectors_in, hamiltonian, block_slots):
    padded = extended(vectors_in, (("rows", 0),), REACH * BLOCK)
    width_local = vectors_in.shape[1]
    stacked = padded.reshape(-1, BLOCK, width_local)
    picked = stacked[block_slots]
    result = jnp.einsum("rkab,rkbv->rav", hamiltonian, picked, precision=lax.Precision.HIGHEST)
    return result.reshape(-1, width_local)


def on_device(hamiltonian, columns, vectors, coefficients):
    block_rows = columns.shape[0]
    total_blocks = block_rows * lax.axis_size("rows")
    row_global = lax.axis_index("rows") * block_rows + jnp.arange(block_rows, dtype=jnp.int32)
    offsets = (columns - row_global[:, None] + REACH) % total_blocks - REACH
    block_slots = jnp.arange(block_rows, dtype=jnp.int32)[:, None] + REACH + offsets
    previous = vectors
    current = apply_operator(vectors, hamiltonian, block_slots)
    filtered = coefficients[0] * previous + coefficients[1] * current
    for order_step in range(2, ORDER + 1):
        following = 2.0 * apply_operator(current, hamiltonian, block_slots) - previous
        filtered = filtered + coefficients[order_step] * following
        previous, current = (current, following)
    total_rows = total_blocks * BLOCK
    stacked_rows = lax.all_to_all(filtered, "vecs", split_axis=0, concat_axis=1, tiled=True)
    partial_value = jnp.dot(
        stacked_rows.T,
        stacked_rows,
        precision=lax.Precision.HIGHEST,
        preferred_element_type=jnp.float32,
    )
    grouped = lax.psum_scatter(partial_value, "vecs", scatter_dimension=0, tiled=True)
    gram = lax.psum_scatter(grouped, "rows", scatter_dimension=1, tiled=True) / total_rows
    return (filtered, gram)


def solution(mesh):
    return jax.shard_map(
        on_device,
        mesh=mesh,
        in_specs=(P("rows", None, None, None), P("rows", None), P("rows", "vecs"), P()),
        out_specs=(P("rows", "vecs"), P("vecs", "rows")),
        check_vma=False,
    )
```

profile of v0, /device:TPU:0, one launch (start us, length us, event | category | flops | bytes accessed | tf_op | source)
XLA Modules:
  0.0 605.5 jit_solution(13704410807666160644)
XLA Ops:
  7.2 1.3 fusion.10
  8.5 3.0 collective-permute-start
  11.5 3.1 collective-permute-start.1
  14.6 0.7 compare_select_fusion
  15.3 0.1 copy.7
  15.4 0.1 reshape.63
  15.5 18.4 %collective-permute-done = f32[512,256]{1,0:T(8,128)S(1)} collective-permute-done((f32[512,256]{1,0:T(8,128)S(1)}, f32[512,256]{1,0:T(8,128)S(1)}, u32[]{:S(2)}, u32[]{:S(2)}) %collective-permute-start) | collective-permute-done | bytes 524320 | tf_op jit(solution)/shard_map/ppermute | solution.py:18
  33.9 2.2 collective-permute-done.1
  36.1 4.9 pad_maximum_fusion
  41.0 14.9 %gather_fusion = f32[192,128,256]{2,1,0:T(8,128)} fusion(f32[40,128,256]{2,1,0:T(8,128)} %bitcast.86, s32[1024]{0:T(1024)S(1)} %pad_clamp_fusion), kind=kCustom, calls=%fused_computation | custom fusion | bytes 50332416 | tf_op jit(solution)/shard_map/gather | solution.py:28
  55.9 19.5 %fusion.12 = f32[32,256,128,1]{1,2,3,0:T(8,128)S(1)} fusion(f32[32,6,128,256]{3,2,1,0:T(8,128)} %bitcast.92, f32[32,6,128,128]{3,2,1,0:T(8,128)} %param.4), kind=kOutput, calls=%fused_computation.42 | convolution fusion | flops 9663676416 | bytes 41943040 | tf_op jit(solution)/shard_map/rkab,rkbv->rav/dot_general | solution.py:29
  75.5 0.1 fusion.9
  75.6 0.3 collective-permute-start.2
  75.9 4.9 collective-permute-start.3
  80.9 16.6 %collective-permute-done.2 = f32[512,256]{1,0:T(8,128)S(1)} collective-permute-done((f32[512,256]{1,0:T(8,128)S(1)}, f32[512,256]{1,0:T(8,128)S(1)}, u32[]{:S(2)}, u32[]{:S(2)}) %collective-permute-start.2) | collective-permute-done | bytes 524320 | tf_op jit(solution)/shard_map/ppermute | solution.py:18
  97.5 4.5 collective-permute-done.3
  101.9 2.7 pad_maximum_fusion.1
  104.7 14.9 %gather_fusion.1 = f32[192,128,256]{2,1,0:T(8,128)} fusion(f32[40,128,256]{2,1,0:T(8,128)} %bitcast.87, s32[1024]{0:T(1024)S(1)} %pad_clamp_fusion), kind=kCustom, calls=%fused_computation.1 | custom fusion | bytes 50332416 | tf_op jit(solution)/shard_map/gather | solution.py:28
  119.6 19.7 %bitcast_multiply_fusion.4 = f32[32,256,128]{1,2,0:T(8,128)S(1)} fusion(f32[32,6,128,256]{3,2,1,0:T(8,128)} %bitcast.93, f32[32,6,128,128]{3,2,1,0:T(8,128)} %param.4), kind=kOutput, calls=%fused_computation.23 | convolution fusion | flops 9664724992 | bytes 41943040 | tf_op jit(solution)/shard_map/rkab,rkbv->rav/dot_general | solution.py:29
  139.3 0.8 bitcast_subtract_fusion.4
  140.2 0.1 fusion.8
  140.2 0.1 collective-permute-start.4
  140.3 4.9 collective-permute-start.5
  145.2 17.9 %collective-permute-done.4 = f32[512,256]{1,0:T(8,128)S(1)} collective-permute-done((f32[512,256]{1,0:T(8,128)S(1)}, f32[512,256]{1,0:T(8,128)S(1)}, u32[]{:S(2)}, u32[]{:S(2)}) %collective-permute-start.4) | collective-permute-done | bytes 524320 | tf_op jit(solution)/shard_map/ppermute | solution.py:18
  163.1 2.9 collective-permute-done.5
  165.9 2.7 pad_maximum_fusion.2
  168.7 14.9 %gather_fusion.2 = f32[192,128,256]{2,1,0:T(8,128)} fusion(f32[40,128,256]{2,1,0:T(8,128)} %bitcast.88, s32[1024]{0:T(1024)S(1)} %pad_clamp_fusion), kind=kCustom, calls=%fused_computation.2 | custom fusion | bytes 50332416 | tf_op jit(solution)/shard_map/gather | solution.py:28
  183.6 19.7 %bitcast_multiply_fusion.3 = f32[32,256,128]{1,2,0:T(8,128)S(1)} fusion(f32[32,6,128,256]{3,2,1,0:T(8,128)} %bitcast.94, f32[32,6,128,128]{3,2,1,0:T(8,128)} %param.4), kind=kOutput, calls=%fused_computation.22 | convolution fusion | flops 9664724992 | bytes 41943040 | tf_op jit(solution)/shard_map/rkab,rkbv->rav/dot_general | solution.py:29
  203.3 1.1 bitcast_subtract_fusion.3
  204.4 0.1 fusion.7
  204.5 0.1 collective-permute-start.6
  204.6 4.9 collective-permute-start.7
  209.5 17.1 %collective-permute-done.6 = f32[512,256]{1,0:T(8,128)S(1)} collective-permute-done((f32[512,256]{1,0:T(8,128)S(1)}, f32[512,256]{1,0:T(8,128)S(1)}, u32[]{:S(2)}, u32[]{:S(2)}) %collective-permute-start.6) | collective-permute-done | bytes 524320 | tf_op jit(solution)/shard_map/ppermute | solution.py:18
  226.6 4.0 collective-permute-done.7
  230.6 2.7 pad_maximum_fusion.3
  233.3 14.9 %gather_fusion.3 = f32[192,128,256]{2,1,0:T(8,128)} fusion(f32[40,128,256]{2,1,0:T(8,128)} %bitcast.89, s32[1024]{0:T(1024)S(1)} %pad_clamp_fusion), kind=kCustom, calls=%fused_computation.3 | custom fusion | bytes 50332416 | tf_op jit(solution)/shard_map/gather | solution.py:28
  248.3 19.7 %bitcast_multiply_fusion.2 = f32[32,256,128]{1,2,0:T(8,128)S(1)} fusion(f32[32,6,128,256]{3,2,1,0:T(8,128)} %bitcast.95, f32[32,6,128,128]{3,2,1,0:T(8,128)} %param.4), kind=kOutput, calls=%fused_computation.21 | convolution fusion | flops 9664724992 | bytes 41943040 | tf_op jit(solution)/shard_map/rkab,rkbv->rav/dot_general | solution.py:29
  268.0 0.8 bitcast_subtract_fusion.2
  268.8 0.1 fusion.6
  268.9 0.1 collective-permute-start.8
  269.0 4.9 collective-permute-start.9
  273.9 17.1 %collective-permute-done.8 = f32[512,256]{1,0:T(8,128)S(1)} collective-permute-done((f32[512,256]{1,0:T(8,128)S(1)}, f32[512,256]{1,0:T(8,128)S(1)}, u32[]{:S(2)}, u32[]{:S(2)}) %collective-permute-start.8) | collective-permute-done | bytes 524320 | tf_op jit(solution)/shard_map/ppermute | solution.py:18
  291.0 2.7 collective-permute-done.9
  293.8 2.7 pad_maximum_fusion.4
  296.5 14.9 %gather_fusion.4 = f32[192,128,256]{2,1,0:T(8,128)} fusion(f32[40,128,256]{2,1,0:T(8,128)} %bitcast.90, s32[1024]{0:T(1024)S(1)} %pad_clamp_fusion), kind=kCustom, calls=%fused_computation.4 | custom fusion | bytes 50332416 | tf_op jit(solution)/shard_map/gather | solution.py:28
  311.4 19.7 %bitcast_multiply_fusion.1 = f32[32,256,128]{1,2,0:T(8,128)S(1)} fusion(f32[32,6,128,256]{3,2,1,0:T(8,128)} %bitcast.96, f32[32,6,128,128]{3,2,1,0:T(8,128)} %param.4), kind=kOutput, calls=%fused_computation.20 | convolution fusion | flops 9664724992 | bytes 41943040 | tf_op jit(solution)/shard_map/rkab,rkbv->rav/dot_general | solution.py:29
  331.2 0.8 bitcast_subtract_fusion.1
  332.0 0.1 fusion.5
  332.1 0.1 collective-permute-start.10
  332.1 5.2 collective-permute-start.11
  337.3 0.7 fusion.11
  338.0 15.5 %collective-permute-done.10 = f32[512,256]{1,0:T(8,128)S(1)} collective-permute-done((f32[512,256]{1,0:T(8,128)S(1)}, f32[512,256]{1,0:T(8,128)S(1)}, u32[]{:S(2)}, u32[]{:S(2)}) %collective-permute-start.10) | collective-permute-done | bytes 524320 | tf_op jit(solution)/shard_map/ppermute | solution.py:18
  353.5 4.9 collective-permute-done.11
  358.3 2.7 pad_maximum_fusion.5
  361.1 14.9 %gather_fusion.5 = f32[192,128,256]{2,1,0:T(8,128)} fusion(f32[40,128,256]{2,1,0:T(8,128)} %bitcast.85, s32[1024]{0:T(1024)S(1)} %pad_clamp_fusion), kind=kCustom, calls=%fused_computation.5 | custom fusion | bytes 50332416 | tf_op jit(solution)/shard_map/gather | solution.py:28
  376.0 22.3 %bitcast_multiply_fusion = f32[32,256,128]{1,2,0:T(8,128)} fusion(f32[32,6,128,256]{3,2,1,0:T(8,128)} %bitcast.91, f32[32,6,128,128]{3,2,1,0:T(8,128)} %param.4), kind=kOutput, calls=%fused_computation.19 | convolution fusion | flops 9664724992 | bytes 41943040 | tf_op jit(solution)/shard_map/rkab,rkbv->rav/dot_general | solution.py:29
  398.3 11.1 %fusion.1 = f32[4096,256]{1,0:T(8,128)S(1)} fusion(f32[4096,256]{1,0:T(8,128)} %copy-done.10, f32[32,256,128]{1,2,0:T(8,128)} %bitcast_multiply_fusion, f32[4096,256]{1,0:T(8,128)} %copy-done.11, f32[4096,256]{1,0:T(8,128)S(1)} %copy-done.8, f32[4096,256]{1,0:T(8,128)S(1)} %copy-done.5, f32[4096,256]{1,0:T(8,128)} %param.6, f32[]{:T(128)} %bitcast.40, ...), kind=kLoop, calls=%fused_computation.14 | loop fusion | flops 14680064 | bytes 33554460 | tf_op jit(solution)/shard_map/add | solution.py:44
  409.5 2.0 copy-done.12
  411.5 51.8 %all_to_all.19 = f32[4,1024,256]{2,1,0:T(8,128)} all-to-all(f32[4,1024,256]{2,1,0:T(8,128)S(1)} %bitcast.100), channel_id=1, replica_groups=mesh['rows'=8,'vecs'=4] {'vecs'}, dimensions={0} | all-to-all | bytes 8388608 | tf_op jit(solution)/shard_map/all_to_all | solution.py:47
  463.3 5.4 copy.8
  468.7 18.2 %fusion.13 = f32[1024,1024]{1,0:T(8,128)} fusion(f32[1024,1024]{0,1:T(8,128)} %bitcast.101), kind=kOutput, calls=%fused_computation.43 | convolution fusion | flops 12884901888 | bytes 8388608 | tf_op jit(solution)/shard_map/dot_general | solution.py:48
  486.9 42.3 %reduce-scatter.3.cloned.1.call-done = f32[256,1024]{1,0:T(8,128)} async-done(((f32[1024,1024]{1,0:T(8,128)}), f32[256,1024]{1,0:T(8,128)}) %reduce-scatter.3.cloned.1.call-update) | async-done | bytes 1048592 | tf_op jit(solution)/shard_map/reduce_scatter | solution.py:54
  529.2 67.7 %reduce-scatter.5.cloned.1.call-done = f32[256,128]{1,0:T(8,128)} async-done(((f32[256,1024]{1,0:T(8,128)}), f32[256,128]{1,0:T(8,128)}) %reduce-scatter.5.cloned.1.call-update) | async-done | bytes 131088 | tf_op jit(solution)/shard_map/reduce_scatter | solution.py:55
  596.9 1.6 broadcast_multiply_fusion
  (33 shorter events, 0.2 us)
Async XLA Ops:
  7.2 522.0 %reduce-scatter.3.cloned.1.call-start = ((), (), s32[]{:S(2)}) async-start(), calls=%async_computation.3 | async-start | bytes 5242880 | tf_op jit(solution)/shard_map/reduce_scatter | solution.py:54
  8.5 25.4 %collective-permute-start = (f32[512,256]{1,0:T(8,128)S(1)}, f32[512,256]{1,0:T(8,128)S(1)}, u32[]{:S(2)}, u32[]{:S(2)}) collective-permute-start(f32[512,256]{1,0:T(8,128)S(1)} %get-tuple-element.12), channel_id=1, source_target_pairs={{0,4},{4,8},{8,12},{12,16},{16,20},{20,24},{24,28},{28,0},{1,5},{5... | collective-permute-start | bytes 1572872 | tf_op jit(solution)/shard_map/ppermute | solution.py:18
  11.5 24.6 %collective-permute-start.1 = (f32[512,256]{1,0:T(8,128)S(1)}, f32[512,256]{1,0:T(8,128)S(1)}, u32[]{:S(2)}, u32[]{:S(2)}) collective-permute-start(f32[512,256]{1,0:T(8,128)S(1)} %get-tuple-element.13), channel_id=1, source_target_pairs={{4,0},{8,4},{12,8},{16,12},{20,16},{24,20},{28,24},{0,28},{5,1},{9... | collective-permute-start | bytes 1572872 | tf_op jit(solution)/shard_map/ppermute | solution.py:19
  75.5 29.2 %copy-start = (f32[32,256,128,1]{1,2,3,0:T(8,128)}, f32[32,256,128,1]{1,2,3,0:T(8,128)S(1)}, u32[]{:S(2)}) copy-start(f32[32,256,128,1]{1,2,3,0:T(8,128)S(1)} %fusion.12) | copy-start | bytes 12582916
  75.6 21.9 %collective-permute-start.2 = (f32[512,256]{1,0:T(8,128)S(1)}, f32[512,256]{1,0:T(8,128)S(1)}, u32[]{:S(2)}, u32[]{:S(2)}) collective-permute-start(f32[512,256]{1,0:T(8,128)S(1)} %bitcast.103), channel_id=1, source_target_pairs={{0,4},{4,8},{8,12},{12,16},{16,20},{20,24},{24,28},{28,0},{1,5},{5... | collective-permute-start | bytes 1572872 | tf_op jit(solution)/shard_map/ppermute | solution.py:18
  75.9 26.0 %collective-permute-start.3 = (f32[512,256]{1,0:T(8,128)S(1)}, f32[512,256]{1,0:T(8,128)S(1)}, u32[]{:S(2)}, u32[]{:S(2)}) collective-permute-start(f32[512,256]{1,0:T(8,128)S(1)} %bitcast.102), channel_id=1, source_target_pairs={{4,0},{8,4},{12,8},{16,12},{20,16},{24,20},{28,24},{0,28},{5,1},{9... | collective-permute-start | bytes 1572872 | tf_op jit(solution)/shard_map/ppermute | solution.py:19
  119.6 19.7 %copy-start.9 = (f32[4096,256]{1,0:T(8,128)S(1)}, f32[4096,256]{1,0:T(8,128)}, u32[]{:S(2)}) copy-start(f32[4096,256]{1,0:T(8,128)} %param.6) | copy-start | bytes 12582916
  140.1 28.5 %copy-start.3 = (f32[4096,256]{1,0:T(8,128)}, f32[4096,256]{1,0:T(8,128)S(1)}, u32[]{:S(2)}) copy-start(f32[4096,256]{1,0:T(8,128)S(1)} %bitcast_subtract_fusion.4) | copy-start | bytes 12582916
  140.2 22.8 %collective-permute-start.4 = (f32[512,256]{1,0:T(8,128)S(1)}, f32[512,256]{1,0:T(8,128)S(1)}, u32[]{:S(2)}, u32[]{:S(2)}) collective-permute-start(f32[512,256]{1,0:T(8,128)S(1)} %get-tuple-element.8), channel_id=1, source_target_pairs={{0,4},{4,8},{8,12},{12,16},{16,20},{20,24},{24,28},{28,0},{1,5},{5... | collective-permute-start | bytes 1572872 | tf_op jit(solution)/shard_map/ppermute | solution.py:18
  140.3 25.6 %collective-permute-start.5 = (f32[512,256]{1,0:T(8,128)S(1)}, f32[512,256]{1,0:T(8,128)S(1)}, u32[]{:S(2)}, u32[]{:S(2)}) collective-permute-start(f32[512,256]{1,0:T(8,128)S(1)} %get-tuple-element.9), channel_id=1, source_target_pairs={{4,0},{8,4},{12,8},{16,12},{20,16},{24,20},{28,24},{0,28},{5,1},{9... | collective-permute-start | bytes 1572872 | tf_op jit(solution)/shard_map/ppermute | solution.py:19
  183.6 19.7 %copy-start.1 = (f32[32,256,128,1]{1,2,3,0:T(8,128)S(1)}, f32[32,256,128,1]{1,2,3,0:T(8,128)}, u32[]{:S(2)}) copy-start(f32[32,256,128,1]{1,2,3,0:T(8,128)} %copy-done) | copy-start | bytes 12582916
  204.4 28.9 %copy-start.6 = (f32[4096,256]{1,0:T(8,128)}, f32[4096,256]{1,0:T(8,128)S(1)}, u32[]{:S(2)}) copy-start(f32[4096,256]{1,0:T(8,128)S(1)} %bitcast_subtract_fusion.3) | copy-start | bytes 12582916
  204.5 22.1 %collective-permute-start.6 = (f32[512,256]{1,0:T(8,128)S(1)}, f32[512,256]{1,0:T(8,128)S(1)}, u32[]{:S(2)}, u32[]{:S(2)}) collective-permute-start(f32[512,256]{1,0:T(8,128)S(1)} %get-tuple-element.6), channel_id=1, source_target_pairs={{0,4},{4,8},{8,12},{12,16},{16,20},{20,24},{24,28},{28,0},{1,5},{5... | collective-permute-start | bytes 1572872 | tf_op jit(solution)/shard_map/ppermute | solution.py:18
  204.6 26.0 %collective-permute-start.7 = (f32[512,256]{1,0:T(8,128)S(1)}, f32[512,256]{1,0:T(8,128)S(1)}, u32[]{:S(2)}, u32[]{:S(2)}) collective-permute-start(f32[512,256]{1,0:T(8,128)S(1)} %get-tuple-element.7), channel_id=1, source_target_pairs={{4,0},{8,4},{12,8},{16,12},{20,16},{24,20},{28,24},{0,28},{5,1},{9... | collective-permute-start | bytes 1572872 | tf_op jit(solution)/shard_map/ppermute | solution.py:19
  248.3 19.7 %copy-start.4 = (f32[4096,256]{1,0:T(8,128)S(1)}, f32[4096,256]{1,0:T(8,128)}, u32[]{:S(2)}) copy-start(f32[4096,256]{1,0:T(8,128)} %copy-done.3) | copy-start | bytes 12582916
  268.8 27.7 %copy-start.10 = (f32[4096,256]{1,0:T(8,128)}, f32[4096,256]{1,0:T(8,128)S(1)}, u32[]{:S(2)}) copy-start(f32[4096,256]{1,0:T(8,128)S(1)} %bitcast_subtract_fusion.2) | copy-start | bytes 12582916
  268.9 22.1 %collective-permute-start.8 = (f32[512,256]{1,0:T(8,128)S(1)}, f32[512,256]{1,0:T(8,128)S(1)}, u32[]{:S(2)}, u32[]{:S(2)}) collective-permute-start(f32[512,256]{1,0:T(8,128)S(1)} %get-tuple-element.4), channel_id=1, source_target_pairs={{0,4},{4,8},{8,12},{12,16},{16,20},{20,24},{24,28},{28,0},{1,5},{5... | collective-permute-start | bytes 1572872 | tf_op jit(solution)/shard_map/ppermute | solution.py:18
  269.0 24.8 %collective-permute-start.9 = (f32[512,256]{1,0:T(8,128)S(1)}, f32[512,256]{1,0:T(8,128)S(1)}, u32[]{:S(2)}, u32[]{:S(2)}) collective-permute-start(f32[512,256]{1,0:T(8,128)S(1)} %get-tuple-element.5), channel_id=1, source_target_pairs={{4,0},{8,4},{12,8},{16,12},{20,16},{24,20},{28,24},{0,28},{5,1},{9... | collective-permute-start | bytes 1572872 | tf_op jit(solution)/shard_map/ppermute | solution.py:19
  311.4 19.7 %copy-start.7 = (f32[4096,256]{1,0:T(8,128)S(1)}, f32[4096,256]{1,0:T(8,128)}, u32[]{:S(2)}) copy-start(f32[4096,256]{1,0:T(8,128)} %copy-done.6) | copy-start | bytes 12582916
  331.2 6.1 %copy-start.13 = (f32[7]{0:T(128)S(1)}, f32[7]{0:T(128)}, u32[]{:S(2)}) copy-start(f32[7]{0:T(128)} %param.7) | copy-start | bytes 88
  332.0 29.1 %copy-start.11 = (f32[4096,256]{1,0:T(8,128)}, f32[4096,256]{1,0:T(8,128)S(1)}, u32[]{:S(2)}) copy-start(f32[4096,256]{1,0:T(8,128)S(1)} %bitcast_subtract_fusion.1) | copy-start | bytes 12582916
  332.1 21.4 %collective-permute-start.10 = (f32[512,256]{1,0:T(8,128)S(1)}, f32[512,256]{1,0:T(8,128)S(1)}, u32[]{:S(2)}, u32[]{:S(2)}) collective-permute-start(f32[512,256]{1,0:T(8,128)S(1)} %get-tuple-element.2), channel_id=1, source_target_pairs={{0,4},{4,8},{8,12},{12,16},{16,20},{20,24},{24,28},{28,0},{1,5},{5... | collective-permute-start | bytes 1572872 | tf_op jit(solution)/shard_map/ppermute | solution.py:18
  332.1 26.2 %collective-permute-start.11 = (f32[512,256]{1,0:T(8,128)S(1)}, f32[512,256]{1,0:T(8,128)S(1)}, u32[]{:S(2)}, u32[]{:S(2)}) collective-permute-start(f32[512,256]{1,0:T(8,128)S(1)} %get-tuple-element.3), channel_id=1, source_target_pairs={{4,0},{8,4},{12,8},{16,12},{20,16},{24,20},{28,24},{0,28},{5,1},{9... | collective-permute-start | bytes 1572872 | tf_op jit(solution)/shard_map/ppermute | solution.py:19
  376.0 22.3 %copy-start.2 = (f32[32,256,128,1]{1,2,3,0:T(8,128)S(1)}, f32[32,256,128,1]{1,2,3,0:T(8,128)}, u32[]{:S(2)}) copy-start(f32[32,256,128,1]{1,2,3,0:T(8,128)} %copy-done) | copy-start | bytes 12582916
  376.0 22.3 %copy-start.5 = (f32[4096,256]{1,0:T(8,128)S(1)}, f32[4096,256]{1,0:T(8,128)}, u32[]{:S(2)}) copy-start(f32[4096,256]{1,0:T(8,128)} %copy-done.3) | copy-start | bytes 12582916
  376.0 22.3 %copy-start.8 = (f32[4096,256]{1,0:T(8,128)S(1)}, f32[4096,256]{1,0:T(8,128)}, u32[]{:S(2)}) copy-start(f32[4096,256]{1,0:T(8,128)} %copy-done.6) | copy-start | bytes 12582916
  409.5 2.0 copy-start.12
  486.9 110.1 %reduce-scatter.5.cloned.1.call-start = ((), (), s32[]{:S(2)}) async-start(), calls=%async_computation.4 | async-start | bytes 1179648 | tf_op jit(solution)/shard_map/reduce_scatter | solution.py:55
Sparse Core Ops, SparseCore 0:
  487.0 42.1 reduce-scatter.2
  533.0 63.9 reduce-scatter.4
where the time goes:
time: 612 us; the launch traced here: 606 us
  waiting for transfers between devices  234 us (38%)
  matrix products  139 us (23%)
  local copies, waits for them, and re-layouts  99.5 us (16%)
  blocking collectives  51.8 us (8%)
  other arithmetic  35.5 us (6%)
  starting transfers between devices  31.5 us (5%)
  between operations  14.5 us (2%)
    dot_general x6, matrix products, apply_operator(): jnp.einsum('rkab,rkbv->rav', hamiltonian, picked, precision=lax.Precision...  121 us
    ppermute x6, waiting for transfers between devices, extended(): before = lax.ppermute(last, axis, up)  103 us
    gather x6, local copies, waits for them, and re-layouts, apply_operator(): picked = stacked[block_slots]  89.6 us
    reduce_scatter x1, waiting for transfers between devices, on_device(): lax.psum_scatter(grouped, 'rows', scatter_dimension=1, tiled=True)  67.7 us
    all_to_all x1, blocking collectives, on_device(): lax.all_to_all(filtered, 'vecs', split_axis=0, concat_axis=1, tiled=True)  51.8 us
    reduce_scatter x1, waiting for transfers between devices, on_device(): lax.psum_scatter(partial_value, 'vecs', scatter_dimension=0, tiled=True)  42.3 us
    ppermute x6, starting transfers between devices, extended(): after = lax.ppermute(initial, axis, down)  27.9 us
    ppermute x6, waiting for transfers between devices, extended(): after = lax.ppermute(initial, axis, down)  21.1 us
  transfers between devices with their start and end apart: 14, of which 14 were waited for; matrix products, arithmetic and copies ran while one was open for 0% of the time, Pallas kernels for 0%

commit v1 on v0

v1 whole, which is shorter than its diff:
```python
import functools

import jax
import jax.numpy as jnp
from jax import lax
from jax.experimental import pallas as pl
from jax.experimental.pallas import tpu as pltpu
from jax.sharding import PartitionSpec as P

BLOCK = 128
REACH = 4
ORDER = 6
LANES = 128
VMEM_BYTES = 32 * 1024 * 1024
F32 = jnp.float32
BF16 = jnp.bfloat16


def params():
    return pltpu.CompilerParams(vmem_limit_bytes=VMEM_BYTES)


def two_parts(x):
    high = x.astype(BF16)
    low = (x - high.astype(F32)).astype(BF16)
    return high, low


def split_kernel(h_ref, out_ref):
    for k in range(h_ref.shape[1]):
        high, low = two_parts(h_ref[0, k])
        out_ref[0, :BLOCK, k * BLOCK : (k + 1) * BLOCK] = high
        out_ref[0, BLOCK:, k * BLOCK : (k + 1) * BLOCK] = low


def split_hamiltonian(hamiltonian):
    rows, per_row = hamiltonian.shape[:2]
    return pl.pallas_call(
        split_kernel,
        grid=(rows,),
        in_specs=[pl.BlockSpec((1, per_row, BLOCK, BLOCK), lambda g: (g, 0, 0, 0))],
        out_specs=pl.BlockSpec((1, 2 * BLOCK, per_row * BLOCK), lambda g: (g, 0, 0)),
        out_shape=jax.ShapeDtypeStruct((rows, 2 * BLOCK, per_row * BLOCK), BF16),
        compiler_params=params(),
        name="split_hamiltonian",
    )(hamiltonian)


def put_parts(parts_ref, start, value):
    high, low = two_parts(value)
    rows = value.shape[0]
    parts_ref[pl.ds(start, rows), :LANES] = high
    parts_ref[pl.ds(start, rows), LANES:] = low


def strip_product(slots_ref, h_ref, parts_ref, strip, base):
    per_row = h_ref.shape[2] // BLOCK
    out = []
    for r in range(REACH):
        picked = []
        for k in range(per_row):
            slot = slots_ref[(strip * REACH + r) * per_row + k] + base
            start = pl.multiple_of(slot * BLOCK, BLOCK)
            picked.append(parts_ref[pl.ds(start, BLOCK), :])
        both = jnp.dot(h_ref[r], jnp.concatenate(picked, axis=0), preferred_element_type=F32)
        top, bottom = both[:BLOCK], both[BLOCK:]
        small = (top[:, LANES:] + bottom[:, :LANES]) + bottom[:, LANES:]
        out.append(top[:, :LANES] + small)
    return out


def interior_kernel(pieces, has_q, slots_ref, scale_ref, h_ref, v_ref, *rest):
    piece_refs, rest = rest[:pieces], rest[pieces:]
    q_ref = rest[0] if has_q else None
    out_ref, parts_ref = rest[-2:]
    step = pl.program_id(0)

    @pl.when(step == 0)
    def _():
        start = 0
        for ref in piece_refs:
            for at in range(0, ref.shape[0], BLOCK):
                put_parts(parts_ref, start, ref[at : at + BLOCK])
                start += BLOCK

    sums = strip_product(slots_ref, h_ref, parts_ref, step + 1, step * REACH)
    for r, total in enumerate(sums):
        rows = slice(r * BLOCK, (r + 1) * BLOCK)
        value = scale_ref[0] * v_ref[rows] + scale_ref[1] * total
        if has_q:
            value = value - q_ref[rows]
        out_ref[rows] = value


def border_kernel(has_q, slots_ref, scale_ref, h_ref, v_ref, *rest):
    strips, rest = rest[:6], rest[6:]
    q_refs = rest[:2] if has_q else None
    outs, parts_ref = rest[-3:-1], rest[-1]
    step = pl.program_id(0)
    last = pl.num_programs(0) - 1
    size = REACH * BLOCK
    for side in range(2):

        @pl.when(step == side * last)
        def _(side=side):
            for n in range(3):
                ref = strips[3 * side + n]
                for at in range(0, size, BLOCK):
                    put_parts(parts_ref, n * size + at, ref[at : at + BLOCK])
            strip = 0 if side == 0 else slots_ref.shape[0] // (REACH * (h_ref.shape[2] // BLOCK)) - 1
            sums = strip_product(slots_ref, h_ref, parts_ref, strip, 0)
            for r, total in enumerate(sums):
                rows = slice(r * BLOCK, (r + 1) * BLOCK)
                value = scale_ref[0] * v_ref[rows] + scale_ref[1] * total
                if has_q:
                    value = value - q_refs[side][rows]
                outs[side][rows] = value


def fixed(shape, index):
    return pl.BlockSpec(shape, lambda g, *_: index)


def interior(slots, scale, parts_h, vectors, chunk, pieces, q):
    strips = parts_h.shape[0] // REACH
    size = REACH * BLOCK
    specs = [
        pl.BlockSpec(memory_space=pltpu.SMEM),
        pl.BlockSpec((REACH, *parts_h.shape[1:]), lambda g, *_: (g + 1, 0, 0)),
        pl.BlockSpec((size, LANES), lambda g, *_: (g + 1, chunk)),
    ]
    args = [scale, parts_h, vectors]
    for array, column in pieces:
        specs.append(fixed((array.shape[0], LANES), (0, column)))
        args.append(array)
    if q is not None:
        specs.append(pl.BlockSpec((size, LANES), lambda g, *_: (g, 0)))
        args.append(q)
    inner = strips - 2
    return pl.pallas_call(
        functools.partial(interior_kernel, len(pieces), q is not None),
        grid_spec=pltpu.PrefetchScalarGridSpec(
            num_scalar_prefetch=1,
            grid=(inner,),
            in_specs=specs,
            out_specs=pl.BlockSpec((size, LANES), lambda g, *_: (g, 0)),
            scratch_shapes=[pltpu.VMEM((strips * size, 2 * LANES), BF16)],
        ),
        out_shape=jax.ShapeDtypeStruct((inner * size, LANES), F32),
        compiler_params=params(),
        cost_estimate=pl.CostEstimate(
            flops=8 * inner * size * LANES * parts_h.shape[2],
            bytes_accessed=2 * parts_h.size + 4 * 5 * inner * size * LANES,
            transcendentals=0,
        ),
        name="interior",
    )(slots, *args)


def border(slots, scale, parts_h, vectors, chunk, strips_in, q):
    strips = parts_h.shape[0] // REACH
    size = REACH * BLOCK
    specs = [
        pl.BlockSpec(memory_space=pltpu.SMEM),
        pl.BlockSpec((REACH, *parts_h.shape[1:]), lambda g, *_: (g * (strips - 1), 0, 0)),
        pl.BlockSpec((size, LANES), lambda g, *_: (g * (strips - 1), chunk)),
    ]
    args = [scale, parts_h, vectors]
    for array, row, column in strips_in:
        specs.append(fixed((size, LANES), (row, column)))
        args.append(array)
    if q is not None:
        specs += [fixed((size, LANES), (0, 0))] * 2
        args += list(q)
    return pl.pallas_call(
        functools.partial(border_kernel, q is not None),
        grid_spec=pltpu.PrefetchScalarGridSpec(
            num_scalar_prefetch=1,
            grid=(2,),
            in_specs=specs,
            out_specs=[fixed((size, LANES), (0, 0))] * 2,
            scratch_shapes=[pltpu.VMEM((3 * size, 2 * LANES), BF16)],
        ),
        out_shape=[jax.ShapeDtypeStruct((size, LANES), F32)] * 2,
        compiler_params=params(),
        cost_estimate=pl.CostEstimate(
            flops=16 * size * LANES * parts_h.shape[2],
            bytes_accessed=2 * parts_h.size // strips * 2 + 4 * 12 * size * LANES,
            transcendentals=0,
        ),
        name="border",
    )(slots, *args)


def gram_kernel(chunks, own_parts, peers, half, has_before, bits_ref, *rest):
    own_refs, rest = rest[: chunks * own_parts], rest[chunks * own_parts :]
    got_refs, rest = rest[: chunks * (peers - 1)], rest[chunks * (peers - 1) :]
    before_ref = rest[0] if has_before else None
    out_ref = rest[-1]
    step = pl.program_id(0)

    @pl.when(step == 0)
    def _():
        out_ref[...] = before_ref[...] if has_before else jnp.zeros_like(out_ref)

    def joined(refs):
        return two_parts(jnp.concatenate([r[...] for r in refs], axis=1))

    own = []
    for c in range(chunks):
        mine = own_refs[c * own_parts : (c + 1) * own_parts]
        own.append(mine[0][...] if own_parts == 1 else jnp.where(step == 0, mine[0][...], mine[1][...]))
    own = jnp.concatenate(own, axis=1)
    high, low = two_parts(own.T)

    def products(other_high, other_low):
        total = jnp.dot(high, other_low, preferred_element_type=F32)
        total += jnp.dot(low, other_high, preferred_element_type=F32)
        return total + jnp.dot(high, other_high, preferred_element_type=F32)

    out_ref[0] += 0.5 * products(*two_parts(own))
    for d in range(1, peers):

        @pl.when(step // half == bits_ref[d.bit_length() - 1])
        def _(d=d):
            out_ref[d] += products(*joined(got_refs[chunks * (d - 1) : chunks * d]))


def gram_sums(bits, own, got, before):
    size = REACH * BLOCK
    chunks, own_parts, peers = len(own), len(own[0]), len(got) + 1
    half = got[0][0].shape[0] // size
    width = chunks * LANES
    specs, args = [], []
    for arrays in own:
        for array in arrays:
            specs.append(pl.BlockSpec((size, LANES), (lambda g, *_: (g, 0)) if own_parts == 1 else (lambda g, *_: (0, 0))))
            args.append(array)
    for arrays in got:
        for array in arrays:
            specs.append(pl.BlockSpec((size, LANES), lambda g, *_: (lax.rem(g, half), 0)))
            args.append(array)
    if before is not None:
        specs.append(fixed(before.shape, (0, 0, 0)))
        args.append(before)
    return pl.pallas_call(
        functools.partial(gram_kernel, chunks, own_parts, peers, half, before is not None),
        grid_spec=pltpu.PrefetchScalarGridSpec(
            num_scalar_prefetch=1,
            grid=(2 * half,),
            in_specs=specs,
            out_specs=fixed((peers, width, width), (0, 0, 0)),
        ),
        out_shape=jax.ShapeDtypeStruct((peers, width, width), F32),
        compiler_params=params(),
        cost_estimate=pl.CostEstimate(
            flops=6 * half * size * width * width * (peers + 1),
            bytes_accessed=4 * (peers + 1) * half * size * width,
            transcendentals=0,
        ),
        name="gram_sums",
    )(bits, *args)


def on_device(hamiltonian, columns, vectors, coefficients):
    block_rows, per_row = columns.shape
    peers = lax.axis_size("rows")
    groups = lax.axis_size("vecs")
    total_blocks = block_rows * peers
    width = vectors.shape[1]
    chunks = width // LANES
    size = REACH * BLOCK
    strips = block_rows // REACH
    rows_at, vecs_at = lax.axis_index("rows"), lax.axis_index("vecs")
    up = [(i, (i + 1) % peers) for i in range(peers)]
    down = [(j, i) for i, j in up]

    def exchange(first, last):
        return lax.ppermute(last, "rows", up), lax.ppermute(first, "rows", down)

    lanes = [slice(c * LANES, (c + 1) * LANES) for c in range(chunks)]
    halo = [exchange(vectors[:size, l], vectors[-size:, l]) for l in lanes]

    local = jnp.arange(block_rows, dtype=jnp.int32)
    offsets = (columns - (rows_at * block_rows + local)[:, None] + REACH) % total_blocks
    slots = (offsets + (local % REACH)[:, None]).reshape(-1)
    parts_h = split_hamiltonian(hamiltonian)

    scales = []
    for step in range(1, ORDER + 1):
        here = coefficients[ORDER - step]
        if step == 2:
            here = here - coefficients[ORDER]
        by = 2.0 * coefficients[ORDER] if step == 1 else (jnp.float32(1.0) if step == ORDER else jnp.float32(2.0))
        scales.append(jnp.stack([here, by]))

    older = [None] * chunks
    terms = [None] * chunks
    inner = [interior(slots, scales[0], parts_h, vectors, c, [(vectors, c)], None) for c in range(chunks)]
    for step in range(1, ORDER + 1):
        for c in range(chunks):
            before, after = halo[c]
            if step == 1:
                edge = [(vectors, 0, c), (vectors, 1, c), (vectors, strips - 2, c), (vectors, strips - 1, c)]
            else:
                low, mid, high = terms[c]
                edge = [(low, 0, 0), (mid, 0, 0), (mid, strips - 3, 0), (high, 0, 0)]
            q = older[c]
            pieces = [(before, 0, 0), *edge, (after, 0, 0)]
            low, high = border(slots, scales[step - 1], parts_h, vectors, c, pieces, q and (q[0], q[2]))
            previous, terms[c] = terms[c], (low, inner[c], high)
            if step < ORDER:
                halo[c] = exchange(low, high)
                next_q = previous and previous[1]
                inner[c] = interior(slots, scales[step], parts_h, vectors, c, [(a, 0) for a in terms[c]], next_q)
            older[c] = previous

    filtered = jnp.concatenate(
        [jnp.concatenate([t[n] for t in terms], axis=1) for n in range(3)], axis=0
    )

    bit_count = (groups - 1).bit_length()
    bits = jnp.stack([(vecs_at >> b) & 1 for b in range(bit_count)]).astype(jnp.int32)

    def swapped(x, distance):
        return lax.ppermute(x, "vecs", [(i, i ^ distance) for i in range(groups)])

    def received(halves_of):
        got = [None] * groups
        for d in range(1, groups):
            if d == 1 or d % 2 == 0:
                bit = bits[d.bit_length() - 1]
                got[d] = [swapped(halves_of(c, bit), d) for c in range(chunks)]
            else:
                got[d] = [swapped(x, 1) for x in got[d - 1]]
        return got[1:]

    half_inner = (strips - 2) * size // 2

    def inner_half(c, bit):
        return lax.dynamic_slice_in_dim(terms[c][1], (1 - bit) * half_inner, half_inner, axis=0)

    def outer_half(c, bit):
        return jnp.where(bit == 0, terms[c][2], terms[c][0])

    sums = gram_sums(bits, [[t[1]] for t in terms], received(inner_half), None)
    sums = gram_sums(bits, [[t[0], t[2]] for t in terms], received(outer_half), sums)

    per_group = peers // groups
    piece = width // per_group
    share = sums.reshape(groups, width, per_group, piece).transpose(0, 2, 1, 3).reshape(groups * per_group, width, piece)
    wanted = rows_at ^ (vecs_at * per_group)
    distance = 1
    while distance < peers:
        share = share.reshape(-1, 2, width, piece)
        mine = (wanted // distance) & 1
        keep = lax.dynamic_index_in_dim(share, mine, axis=1, keepdims=False)
        send = lax.dynamic_index_in_dim(share, 1 - mine, axis=1, keepdims=False)
        share = keep + lax.ppermute(send, "rows", [(i, i ^ distance) for i in range(peers)])
        distance *= 2
    share = share.reshape(per_group, piece, piece)
    turned = [None] * per_group
    for n in range(per_group):
        tile = (rows_at + n) % per_group
        pairs = []
        for i in range(peers):
            for g in range(groups):
                to = (g * per_group + (i + n) % per_group) * groups + i // per_group
                pairs.append((i * groups + g, to))
        sent = lax.dynamic_index_in_dim(share, tile, axis=0, keepdims=False)
        turned[n] = lax.ppermute(sent, ("rows", "vecs"), pairs).T
    gram = []
    for t in range(per_group):
        which = (rows_at - t) % per_group
        gram.append(share[t] + lax.dynamic_index_in_dim(jnp.stack(turned), which, axis=0, keepdims=False))
    gram = jnp.concatenate(gram, axis=0) / (total_blocks * BLOCK)
    return filtered, gram


def solution(mesh):
    return jax.shard_map(
        on_device,
        mesh=mesh,
        in_specs=(P("rows", None, None, None), P("rows", None), P("rows", "vecs"), P()),
        out_specs=(P("rows", "vecs"), P("vecs", "rows")),
        check_vma=False,
    )
```

time: 612 us -> 310 us (0.51)
  waiting for transfers between devices: 234 us -> 49.2 us
  matrix products: 139 us -> 0 us
  Pallas kernels: 0 us -> 127 us
  local copies, waits for them, and re-layouts: 99.5 us -> 41.7 us
  blocking collectives: 51.8 us -> 0 us
  starting transfers between devices: 31.5 us -> 70 us
  other arithmetic: 35.5 us -> 12.8 us
  between operations: 14.5 us -> 3.1 us
    dot_general x7 -> x0, matrix products: 139 us -> none  [the longest x6 121 us: apply_operator(): jnp.einsum('rkab,rkbv->rav', hamiltonian, picked, precision=lax.Precision...]
    pallas_call x0 -> x27, Pallas kernels: none -> 127 us  [the longest x12 62.9 us: interior(): pl.pallas_call(functools.partial(interior_kernel, len(pieces), q is not N...]
    reduce_scatter x2 -> x0, waiting for transfers between devices: 110 us -> none  [the longest x1 67.7 us: on_device(): lax.psum_scatter(grouped, 'rows', scatter_dimension=1, tiled=True)]
    gather x6 -> x0, local copies, waits for them, and re-layouts: 89.6 us -> none  [apply_operator(): picked = stacked[block_slots]]
    ppermute x12 -> x41, waiting for transfers between devices: 124 us -> 49.2 us  [the longest x3 25.9 us: on_device(): lax.ppermute(send, 'rows', [(i, i ^ distance) for i in range(peers)])]
    all_to_all x1 -> x0, blocking collectives: 51.8 us -> none  [on_device(): lax.all_to_all(filtered, 'vecs', split_axis=0, concat_axis=1, tiled=True)]
    ppermute x12 -> x41, starting transfers between devices: 31.5 us -> 70 us  [the longest x24 57.8 us: exchange(): return (lax.ppermute(last, 'rows', up), lax.ppermute(first, 'rows', down))]
    unnamed x28 -> x50, local copies, waits for them, and re-layouts: 2.06 us -> 24.4 us
  transfers between devices with their start and end apart: 14 -> 41, of which waited for: 14 -> 10; matrix products, arithmetic and copies ran while one was open for 0% -> 4% of each run, Pallas kernels for 0% -> 41%
where the time goes in v1:
time: 310 us; the launch traced here: 304 us
  Pallas kernels  127 us (41%)
  starting transfers between devices  70 us (23%)
  waiting for transfers between devices  49.2 us (16%)
  local copies, waits for them, and re-layouts  41.7 us (13%)
  other arithmetic  12.8 us (4%)
  between operations  3.1 us (1%)
    pallas_call x12, Pallas kernels, interior(): pl.pallas_call(functools.partial(interior_kernel, len(pieces), q is not N...  62.9 us
    ppermute x24, starting transfers between devices, exchange(): return (lax.ppermute(last, 'rows', up), lax.ppermute(first, 'rows', down))  57.8 us
    pallas_call x12, Pallas kernels, border(): pl.pallas_call(functools.partial(border_kernel, q is not None), grid_spec...  33.1 us
    ppermute x3, waiting for transfers between devices, on_device(): lax.ppermute(send, 'rows', [(i, i ^ distance) for i in range(peers)])  25.9 us
    unnamed x50, local copies, waits for them, and re-layouts  24.4 us
    pallas_call x1, Pallas kernels, split_hamiltonian(): pl.pallas_call(split_kernel, grid=(rows,), in_specs=[pl.BlockSpec((1, per...  18 us
    ppermute x24, waiting for transfers between devices, exchange(): return (lax.ppermute(last, 'rows', up), lax.ppermute(first, 'rows', down))  13.7 us
    pallas_call x2, Pallas kernels, gram_sums(): pl.pallas_call(functools.partial(gram_kernel, chunks, own_parts, peers, h...  13.1 us
  transfers between devices with their start and end apart: 41, of which 10 were waited for; matrix products, arithmetic and copies ran while one was open for 4% of the time, Pallas kernels for 41%

profile of v1, /device:TPU:0, one launch (start us, length us, event | category | flops | bytes accessed | tf_op | source)
XLA Modules:
  0.0 304.1 jit_solution(7679794505906608774)
XLA Ops:
  0.6 2.0 fusion.8
  2.7 6.0 %collective-permute-start.1 = (f32[512,128]{1,0:T(8,128)}, f32[512,128]{1,0:T(8,128)S(1)}, u32[]{:S(2)}, u32[]{:S(2)}) collective-permute-start(f32[512,128]{1,0:T(8,128)} %get-tuple-element.50), channel_id=1, source_target_pairs={{4,0},{8,4},{12,8},{16,12},{20,16},{24,20},{28,24},{0,28},{5,1},{9... | collective-permute-start | bytes 786440 | tf_op jit(solution)/shard_map/ppermute | solution.py:279
  9.2 1.5 collective-permute-start.12
  10.7 1.6 fusion.9
  17.2 18.0 %split_hamiltonian.1.h_ref = bf16[32,256,768]{2,1,0:T(8,128)(2,1)S(1)} custom-call(f32[32,6,128,128]{3,2,1,0:T(8,128)} %h_ref.1), custom_call_target="tpu_custom_call" | custom-call | tf_op jit(solution)/shard_map/split_hamiltonian/pallas_call | solution.py:38
  36.0 5.2 %interior.17.rest_2_.rest_3_.rest_1_ = f32[3072,128]{1,0:T(8,128)S(1)} custom-call(s32[192]{0:T(256)S(1)} %reshape.49.slots_ref, f32[2]{0:T(128)S(1)} %pad_maximum_fusion.5.scale_ref, bf16[32,256,768]{2,1,0:T(8,128)(2,1)S(1)} %split_hamiltonian.1.h_ref, f32[4096,256]{1,0:T(8,128)S(1)} %copy-done.3, f32[4096,256]{1,0:T(8,128)S(1)} %copy-done.3), custom_call_target="tpu_custom_call" | custom-call | flops 2415919104 | bytes 20447232 | tf_op jit(solution)/shard_map/interior/pallas_call | solution.py:140
  42.0 4.6 %copy-done.1 = bf16[32,256,768]{2,1,0:T(8,128)(2,1)S(1)} copy-done((bf16[32,256,768]{2,1,0:T(8,128)(2,1)S(1)}, bf16[32,256,768]{2,1,0:T(8,128)(2,1)}, u32[]{:S(2)}) %copy-start.1) | copy-done | bytes 12582936
  46.6 2.2 copy-done.4
  48.8 5.2 %interior.12.rest_2_.rest_3_.rest_1_ = f32[3072,128]{1,0:T(8,128)S(1)} custom-call(s32[192]{0:T(256)S(1)} %reshape.49.slots_ref, f32[2]{0:T(128)S(1)} %pad_maximum_fusion.5.scale_ref, bf16[32,256,768]{2,1,0:T(8,128)(2,1)S(1)} %copy-done.1, f32[4096,256]{1,0:T(8,128)S(1)} %copy-done.4, f32[4096,256]{1,0:T(8,128)S(1)} %copy-done.4), custom_call_target="tpu_custom_call" | custom-call | flops 2415919104 | bytes 20447232 | tf_op jit(solution)/shard_map/interior/pallas_call | solution.py:140
  54.0 2.6 border.12
  56.8 4.7 %collective-permute-start.3 = (f32[512,128]{1,0:T(8,128)S(1)}, f32[512,128]{1,0:T(8,128)S(1)}, u32[]{:S(2)}, u32[]{:S(2)}) collective-permute-start(f32[512,128]{1,0:T(8,128)S(1)} %get-tuple-element.27.rest_1_.rest_0_.rest_6_), channel_id=1, source_target_pairs={{4,0},{8,4},{12,8},{16,12},{20,16},{24,20},{28,24},{0,28},{5,1},{9... | collective-permute-start | bytes 786440 | tf_op jit(solution)/shard_map/ppermute | solution.py:279
  61.5 2.6 border.18
  64.2 4.7 %collective-permute-start.15 = (f32[512,128]{1,0:T(8,128)S(1)}, f32[512,128]{1,0:T(8,128)S(1)}, u32[]{:S(2)}, u32[]{:S(2)}) collective-permute-start(f32[512,128]{1,0:T(8,128)S(1)} %get-tuple-element.38.rest_1_.rest_0_.rest_6_), channel_id=1, source_target_pairs={{4,0},{8,4},{12,8},{16,12},{20,16},{24,20},{28,24},{0,28},{5,1},{9... | collective-permute-start | bytes 786440 | tf_op jit(solution)/shard_map/ppermute | solution.py:279
  68.9 5.2 %interior.13.rest_2_.rest_3_.rest_1_ = f32[3072,128]{1,0:T(8,128)S(1)} custom-call(s32[192]{0:T(256)S(1)} %reshape.49.slots_ref, f32[2]{0:T(128)S(1)} %pad_maximum_fusion.scale_ref, bf16[32,256,768]{2,1,0:T(8,128)(2,1)S(1)} %copy-done.1, f32[4096,256]{1,0:T(8,128)S(1)} %copy-done.5, f32[512,128]{1,0:T(8,128)S(1)} %get-tuple-element.27.rest_1_.rest_0_.rest_6_, ...), custom_call_target="tpu_custom_call" | custom-call | flops 2415919104 | bytes 20447232 | tf_op jit(solution)/shard_map/interior/pallas_call | solution.py:140
  74.1 5.2 %interior.18.rest_2_.rest_3_.rest_1_ = f32[3072,128]{1,0:T(8,128)S(1)} custom-call(s32[192]{0:T(256)S(1)} %reshape.49.slots_ref, f32[2]{0:T(128)S(1)} %pad_maximum_fusion.scale_ref, bf16[32,256,768]{2,1,0:T(8,128)(2,1)S(1)} %copy-done.1, f32[4096,256]{1,0:T(8,128)S(1)} %copy-done.5, f32[512,128]{1,0:T(8,128)S(1)} %get-tuple-element.38.rest_1_.rest_0_.rest_6_, ...), custom_call_target="tpu_custom_call" | custom-call | flops 2415919104 | bytes 20447232 | tf_op jit(solution)/shard_map/interior/pallas_call | solution.py:140
  79.3 1.5 collective-permute-done.15.rest_5_
  80.9 2.6 border.19
  83.8 4.5 %collective-permute-start.17 = (f32[512,128]{1,0:T(8,128)S(1)}, f32[512,128]{1,0:T(8,128)S(1)}, u32[]{:S(2)}, u32[]{:S(2)}) collective-permute-start(f32[512,128]{1,0:T(8,128)S(1)} %get-tuple-element.40.rest_1_.rest_0_.rest_6_), channel_id=1, source_target_pairs={{4,0},{8,4},{12,8},{16,12},{20,16},{24,20},{28,24},{0,28},{5,1},{9... | collective-permute-start | bytes 786440 | tf_op jit(solution)/shard_map/ppermute | solution.py:279
  88.3 2.6 border.13
  91.0 4.7 %collective-permute-start.5 = (f32[512,128]{1,0:T(8,128)S(1)}, f32[512,128]{1,0:T(8,128)S(1)}, u32[]{:S(2)}, u32[]{:S(2)}) collective-permute-start(f32[512,128]{1,0:T(8,128)S(1)} %get-tuple-element.29.rest_1_.rest_0_.rest_6_), channel_id=1, source_target_pairs={{4,0},{8,4},{12,8},{16,12},{20,16},{24,20},{28,24},{0,28},{5,1},{9... | collective-permute-start | bytes 786440 | tf_op jit(solution)/shard_map/ppermute | solution.py:279
  95.7 5.2 %interior.14.rest_2_.rest_3_.rest_1_ = f32[3072,128]{1,0:T(8,128)S(1)} custom-call(s32[192]{0:T(256)S(1)} %reshape.49.slots_ref, f32[2]{0:T(128)S(1)} %pad_maximum_fusion.1.scale_ref, bf16[32,256,768]{2,1,0:T(8,128)(2,1)S(1)} %copy-done.1, f32[4096,256]{1,0:T(8,128)S(1)} %copy-done.5, f32[512,128]{1,0:T(8,128)S(1)} %get-tuple-element.29.rest_1_.rest_0_.rest_6_, ...), custom_call_target="tpu_custom_call" | custom-call | flops 2415919104 | bytes 20447232 | tf_op jit(solution)/shard_map/interior/pallas_call | solution.py:140
  100.9 5.2 %interior.19.rest_2_.rest_3_.rest_1_ = f32[3072,128]{1,0:T(8,128)S(1)} custom-call(s32[192]{0:T(256)S(1)} %reshape.49.slots_ref, f32[2]{0:T(128)S(1)} %pad_maximum_fusion.1.scale_ref, bf16[32,256,768]{2,1,0:T(8,128)(2,1)S(1)} %copy-done.1, f32[4096,256]{1,0:T(8,128)S(1)} %copy-done.5, f32[512,128]{1,0:T(8,128)S(1)} %get-tuple-element.40.rest_1_.rest_0_.rest_6_, ...), custom_call_target="tpu_custom_call" | custom-call | flops 2415919104 | bytes 20447232 | tf_op jit(solution)/shard_map/interior/pallas_call | solution.py:140
  106.1 2.4 collective-permute-done.5.rest_5_
  108.5 2.6 border.14
  111.2 4.7 %collective-permute-start.7 = (f32[512,128]{1,0:T(8,128)S(1)}, f32[512,128]{1,0:T(8,128)S(1)}, u32[]{:S(2)}, u32[]{:S(2)}) collective-permute-start(f32[512,128]{1,0:T(8,128)S(1)} %get-tuple-element.31.rest_1_.rest_0_.rest_6_), channel_id=1, source_target_pairs={{4,0},{8,4},{12,8},{16,12},{20,16},{24,20},{28,24},{0,28},{5,1},{9... | collective-permute-start | bytes 786440 | tf_op jit(solution)/shard_map/ppermute | solution.py:279
  116.0 2.6 border.20
  118.6 4.7 %collective-permute-start.19 = (f32[512,128]{1,0:T(8,128)S(1)}, f32[512,128]{1,0:T(8,128)S(1)}, u32[]{:S(2)}, u32[]{:S(2)}) collective-permute-start(f32[512,128]{1,0:T(8,128)S(1)} %get-tuple-element.42.rest_1_.rest_0_.rest_6_), channel_id=1, source_target_pairs={{4,0},{8,4},{12,8},{16,12},{20,16},{24,20},{28,24},{0,28},{5,1},{9... | collective-permute-start | bytes 786440 | tf_op jit(solution)/shard_map/ppermute | solution.py:279
  123.4 5.2 %interior.15.rest_2_.rest_3_.rest_1_ = f32[3072,128]{1,0:T(8,128)S(1)} custom-call(s32[192]{0:T(256)S(1)} %reshape.49.slots_ref, f32[2]{0:T(128)S(1)} %pad_maximum_fusion.2.scale_ref, bf16[32,256,768]{2,1,0:T(8,128)(2,1)S(1)} %copy-done.1, f32[4096,256]{1,0:T(8,128)S(1)} %copy-done.5, f32[512,128]{1,0:T(8,128)S(1)} %get-tuple-element.31.rest_1_.rest_0_.rest_6_, ...), custom_call_target="tpu_custom_call" | custom-call | flops 2415919104 | bytes 20447232 | tf_op jit(solution)/shard_map/interior/pallas_call | solution.py:140
  128.6 5.2 %interior.20.rest_2_.rest_3_.rest_1_ = f32[3072,128]{1,0:T(8,128)S(1)} custom-call(s32[192]{0:T(256)S(1)} %reshape.49.slots_ref, f32[2]{0:T(128)S(1)} %pad_maximum_fusion.2.scale_ref, bf16[32,256,768]{2,1,0:T(8,128)(2,1)S(1)} %copy-done.1, f32[4096,256]{1,0:T(8,128)S(1)} %copy-done.5, f32[512,128]{1,0:T(8,128)S(1)} %get-tuple-element.42.rest_1_.rest_0_.rest_6_, ...), custom_call_target="tpu_custom_call" | custom-call | flops 2415919104 | bytes 20447232 | tf_op jit(solution)/shard_map/interior/pallas_call | solution.py:140
  133.8 2.6 border.15
  136.5 4.7 %collective-permute-start.9 = (f32[512,128]{1,0:T(8,128)S(1)}, f32[512,128]{1,0:T(8,128)S(1)}, u32[]{:S(2)}, u32[]{:S(2)}) collective-permute-start(f32[512,128]{1,0:T(8,128)S(1)} %get-tuple-element.33.rest_1_.rest_0_.rest_6_), channel_id=1, source_target_pairs={{4,0},{8,4},{12,8},{16,12},{20,16},{24,20},{28,24},{0,28},{5,1},{9... | collective-permute-start | bytes 786440 | tf_op jit(solution)/shard_map/ppermute | solution.py:279
  141.2 2.6 border.21
  143.9 6.4 %collective-permute-start.21 = (f32[512,128]{1,0:T(8,128)S(1)}, f32[512,128]{1,0:T(8,128)S(1)}, u32[]{:S(2)}, u32[]{:S(2)}) collective-permute-start(f32[512,128]{1,0:T(8,128)S(1)} %get-tuple-element.44.rest_1_.rest_0_.rest_6_), channel_id=1, source_target_pairs={{4,0},{8,4},{12,8},{16,12},{20,16},{24,20},{28,24},{0,28},{5,1},{9... | collective-permute-start | bytes 786440 | tf_op jit(solution)/shard_map/ppermute | solution.py:279
  150.3 5.2 %interior.16.rest_2_.rest_3_.rest_1_ = f32[3072,128]{1,0:T(8,128)S(1)} custom-call(s32[192]{0:T(256)S(1)} %reshape.49.slots_ref, f32[2]{0:T(128)S(1)} %pad_maximum_fusion.3.scale_ref, bf16[32,256,768]{2,1,0:T(8,128)(2,1)S(1)} %copy-done.1, f32[4096,256]{1,0:T(8,128)S(1)} %copy-done.5, f32[512,128]{1,0:T(8,128)S(1)} %get-tuple-element.33.rest_1_.rest_0_.rest_6_, ...), custom_call_target="tpu_custom_call" | custom-call | flops 2415919104 | bytes 20447232 | tf_op jit(solution)/shard_map/interior/pallas_call | solution.py:140
  155.5 5.2 %interior.21.rest_2_.rest_3_.rest_1_ = f32[3072,128]{1,0:T(8,128)S(1)} custom-call(s32[192]{0:T(256)S(1)} %reshape.49.slots_ref, f32[2]{0:T(128)S(1)} %pad_maximum_fusion.3.scale_ref, bf16[32,256,768]{2,1,0:T(8,128)(2,1)S(1)} %copy-done.1, f32[4096,256]{1,0:T(8,128)S(1)} %copy-done.5, f32[512,128]{1,0:T(8,128)S(1)} %get-tuple-element.44.rest_1_.rest_0_.rest_6_, ...), custom_call_target="tpu_custom_call" | custom-call | flops 2415919104 | bytes 20447232 | tf_op jit(solution)/shard_map/interior/pallas_call | solution.py:140
  160.8 3.3 %border.22 = (f32[512,128]{1,0:T(8,128)S(1)}, f32[512,128]{1,0:T(8,128)}) custom-call(s32[192]{0:T(256)S(1)} %reshape.49.slots_ref, f32[2]{0:T(128)S(1)} %pad_maximum_fusion.3.scale_ref, bf16[32,256,768]{2,1,0:T(8,128)(2,1)S(1)} %copy-done.1, f32[4096,256]{1,0:T(8,128)S(1)} %copy-done.5, f32[512,128]{1,0:T(8,128)S(1)} %collective-permute-done.20.rest_0_, ...), custom_call_target="tpu_custom_call" | custom-call | flops 805306368 | bytes 6291456 | tf_op jit(solution)/shard_map/border/pallas_call | solution.py:175
  164.1 5.6 %interior.23.rest_1_ = f32[3072,128]{1,0:T(8,128)S(1)} custom-call(s32[192]{0:T(256)S(1)} %reshape.49.slots_ref, f32[2]{0:T(128)S(1)} %pad_maximum_fusion.4.scale_ref, bf16[32,256,768]{2,1,0:T(8,128)(2,1)S(1)} %copy-done.1, f32[4096,256]{1,0:T(8,128)S(1)} %copy-done.5, f32[512,128]{1,0:T(8,128)S(1)} %get-tuple-element.46.rest_1_.rest_0_, ...), custom_call_target="tpu_custom_call" | custom-call | flops 2415919104 | bytes 20447232 | tf_op jit(solution)/shard_map/interior/pallas_call | solution.py:140
  172.1 1.5 collective-permute-start.33
  173.6 2.6 border.16
  176.3 5.2 %interior.22.rest_0_ = f32[3072,128]{1,0:T(8,128)S(1)} custom-call(s32[192]{0:T(256)S(1)} %reshape.49.slots_ref, f32[2]{0:T(128)S(1)} %pad_maximum_fusion.4.scale_ref, bf16[32,256,768]{2,1,0:T(8,128)(2,1)S(1)} %copy-done.1, f32[4096,256]{1,0:T(8,128)S(1)} %copy-done.5, f32[512,128]{1,0:T(8,128)S(1)} %get-tuple-element.35.rest_1_.rest_0_, ...), custom_call_target="tpu_custom_call" | custom-call | flops 2415919104 | bytes 20447232 | tf_op jit(solution)/shard_map/interior/pallas_call | solution.py:140
  184.4 4.7 %collective-permute-start.11 = (f32[512,128]{1,0:T(8,128)S(1)}, f32[512,128]{1,0:T(8,128)}, u32[]{:S(2)}, u32[]{:S(2)}) collective-permute-start(f32[512,128]{1,0:T(8,128)S(1)} %get-tuple-element.35.rest_1_.rest_0_), channel_id=1, source_target_pairs={{4,0},{8,4},{12,8},{16,12},{20,16},{24,20},{28,24},{0,28},{5,1},{9... | collective-permute-start | bytes 786440 | tf_op jit(solution)/shard_map/ppermute | solution.py:279
  189.1 9.4 %collective-permute-done.10.rest_0_ = f32[512,128]{1,0:T(8,128)} collective-permute-done((f32[512,128]{1,0:T(8,128)S(1)}, f32[512,128]{1,0:T(8,128)}, u32[]{:S(2)}, u32[]{:S(2)}) %collective-permute-start.10) | collective-permute-done | bytes 262176 | tf_op jit(solution)/shard_map/ppermute | solution.py:279
  198.6 5.1 %collective-permute-start.23 = (f32[512,128]{1,0:T(8,128)S(1)}, f32[512,128]{1,0:T(8,128)S(1)}, u32[]{:S(2)}, u32[]{:S(2)}) collective-permute-start(f32[512,128]{1,0:T(8,128)S(1)} %get-tuple-element.46.rest_1_.rest_0_), channel_id=1, source_target_pairs={{4,0},{8,4},{12,8},{16,12},{20,16},{24,20},{28,24},{0,28},{5,1},{9... | collective-permute-start | bytes 786440 | tf_op jit(solution)/shard_map/ppermute | solution.py:279
  203.9 4.6 %copy-done.2 = bf16[32,256,768]{2,1,0:T(8,128)(2,1)S(1)} copy-done((bf16[32,256,768]{2,1,0:T(8,128)(2,1)S(1)}, bf16[32,256,768]{2,1,0:T(8,128)(2,1)}, u32[]{:S(2)}) %copy-start.2) | copy-done | bytes 12582936
  208.5 2.2 copy-done.6
  214.0 3.1 %border.17 = (f32[512,128]{1,0:T(8,128)S(1)}, f32[512,128]{1,0:T(8,128)S(1)}) custom-call(s32[192]{0:T(256)S(1)} %reshape.49.slots_ref, f32[2]{0:T(128)S(1)} %pad_maximum_fusion.4.scale_ref, bf16[32,256,768]{2,1,0:T(8,128)(2,1)S(1)} %copy-done.2, f32[4096,256]{1,0:T(8,128)S(1)} %copy-done.6, f32[512,128]{1,0:T(8,128)} %collective-permute-done.10.rest_0_, ...), custom_call_target="tpu_custom_call" | custom-call | flops 805306368 | bytes 6291456 | tf_op jit(solution)/shard_map/border/pallas_call | solution.py:175
  219.0 1.5 collective-permute-start.26
  220.5 3.1 %border.23 = (f32[512,128]{1,0:T(8,128)S(1)}, f32[512,128]{1,0:T(8,128)S(1)}) custom-call(s32[192]{0:T(256)S(1)} %reshape.49.slots_ref, f32[2]{0:T(128)S(1)} %pad_maximum_fusion.4.scale_ref, bf16[32,256,768]{2,1,0:T(8,128)(2,1)S(1)} %copy-done.2, f32[4096,256]{1,0:T(8,128)S(1)} %copy-done.6, f32[512,128]{1,0:T(8,128)} %collective-permute-done.22.rest_0_, ...), custom_call_target="tpu_custom_call" | custom-call | flops 805306368 | bytes 6291456 | tf_op jit(solution)/shard_map/border/pallas_call | solution.py:175
  223.7 3.7 %collective-permute-done.26.rest_6_ = f32[512,128]{1,0:T(8,128)} collective-permute-done((f32[512,128]{1,0:T(8,128)S(1)}, f32[512,128]{1,0:T(8,128)}, u32[]{:S(2)}, u32[]{:S(2)}) %collective-permute-start.26) | collective-permute-done | bytes 262176 | tf_op jit(solution)/shard_map/ppermute | solution.py:326
  227.4 1.5 collective-permute-start.27
  229.0 5.9 %collective-permute-done.27.rest_7_ = f32[512,128]{1,0:T(8,128)S(1)} collective-permute-done((f32[512,128]{1,0:T(8,128)S(1)}, f32[512,128]{1,0:T(8,128)S(1)}, u32[]{:S(2)}, u32[]{:S(2)}) %collective-permute-start.27) | collective-permute-done | bytes 262176 | tf_op jit(solution)/shard_map/ppermute | solution.py:326
  235.9 1.4 copy-done.10
  238.7 9.4 %gram_sums.2.rest_10_ = f32[4,256,256]{2,1,0:T(8,128)S(1)} custom-call(s32[2]{0:T(128)S(1)} %pad_add_fusion.bits_ref, f32[3072,128]{1,0:T(8,128)S(1)} %copy-done.13, f32[3072,128]{1,0:T(8,128)S(1)} %copy-done.10, f32[1536,128]{1,0:T(8,128)} %collective-permute-done.30.rest_2_, f32[1536,128]{1,0:T(8,128)} %collective-permute-done.31.rest_3_, ...), custom_call_target="tpu_custom_call" | custom-call | flops 3019898880 | bytes 7864320 | tf_op jit(solution)/shard_map/gram_sums/pallas_call | solution.py:246
  248.2 3.7 %gram_sums.3 = f32[4,256,256]{2,1,0:T(8,128)S(1)} custom-call(s32[2]{0:T(128)S(1)} %pad_add_fusion.bits_ref, f32[512,128]{1,0:T(8,128)S(1)} %get-tuple-element.36.rest_0_, f32[512,128]{1,0:T(8,128)S(1)} %get-tuple-element.48.rest_1_, f32[512,128]{1,0:T(8,128)S(1)} %get-tuple-element.47.rest_2_, f32[512,128]{1,0:T(8,128)S(1)} %get-tuple-element.49.rest_3_, ...), custom_call_target="tpu_custom_call" | custom-call | flops 1006632960 | bytes 2621440 | tf_op jit(solution)/shard_map/gram_sums/pallas_call | solution.py:246
  252.9 2.9 reshape.50
  255.7 3.6 %constant_dynamic-slice_fusion.3 = (f32[4,256,1,128]{3,2,1,0:T(1,128)}, f32[4,256,1,128]{3,2,1,0:T(1,128)}) fusion(f32[4,256,2,128]{3,2,1,0:T(2,128)} %reshape.50, s32[]{:T(128)S(6)} %select_n.114, s32[]{:T(128)S(6)} %select_n.113), kind=kLoop, calls=%fused_computation.27 | loop fusion | bytes 2097160 | tf_op jit(solution)/shard_map/dynamic-slice.1
  259.3 13.9 %collective-permute-done.36 = f32[4,256,128]{2,1,0:T(8,128)} collective-permute-done((f32[4,256,128]{2,1,0:T(8,128)}, f32[4,256,128]{2,1,0:T(8,128)}, u32[]{:S(2)}, u32[]{:S(2)}) %collective-permute-start.36) | collective-permute-done | bytes 524320 | tf_op jit(solution)/shard_map/ppermute | solution.py:359
  276.0 1.5 collective-permute-start.37
  277.5 5.9 %collective-permute-done.37 = f32[2,256,128]{2,1,0:T(8,128)} collective-permute-done((f32[2,256,128]{2,1,0:T(8,128)}, f32[2,256,128]{2,1,0:T(8,128)}, u32[]{:S(2)}, u32[]{:S(2)}) %collective-permute-start.37) | collective-permute-done | bytes 262176 | tf_op jit(solution)/shard_map/ppermute | solution.py:359
  286.5 6.1 %collective-permute-done.38 = f32[1,256,128]{2,1,0:T(8,128)} collective-permute-done((f32[1,256,128]{2,1,0:T(8,128)S(1)}, f32[1,256,128]{2,1,0:T(8,128)}, u32[]{:S(2)}, u32[]{:S(2)}) %collective-permute-start.38) | collective-permute-done | bytes 131104 | tf_op jit(solution)/shard_map/ppermute | solution.py:359
  294.3 1.6 copy.10
  295.8 1.6 copy.9
  297.4 1.5 collective-permute-start.39
  299.6 3.6 %maximum_maximum_fusion = f32[4096,256]{1,0:T(8,128)} fusion(f32[512,128]{1,0:T(8,128)} %copy-done.18, f32[512,128]{1,0:T(8,128)} %copy-done.16, f32[3072,128]{1,0:T(8,128)S(1)} %copy-done.11, f32[3072,128]{1,0:T(8,128)S(1)} %copy-done.14, f32[512,128]{1,0:T(8,128)} %copy-done.17, f32[512,128]{1,0:T(8,128)S(1)} %get-tuple-element.36.rest_0_), kind=kLoop, calls=%fused_computation | loop fusion | flops 5242880 | bytes 8388608 | tf_op jit(solution)/shard_map/concatenate | solution.py:318
  (125 shorter events, 29.1 us)
Async XLA Ops:
  2.7 51.3 %collective-permute-start.1 = (f32[512,128]{1,0:T(8,128)}, f32[512,128]{1,0:T(8,128)S(1)}, u32[]{:S(2)}, u32[]{:S(2)}) collective-permute-start(f32[512,128]{1,0:T(8,128)} %get-tuple-element.50), channel_id=1, source_target_pairs={{4,0},{8,4},{12,8},{16,12},{20,16},{24,20},{28,24},{0,28},{5,1},{9... | collective-permute-start | bytes 786440 | tf_op jit(solution)/shard_map/ppermute | solution.py:279
  8.7 52.9 %collective-permute-start.13 = (f32[512,128]{1,0:T(8,128)}, f32[512,128]{1,0:T(8,128)S(1)}, u32[]{:S(2)}, u32[]{:S(2)}) collective-permute-start(f32[512,128]{1,0:T(8,128)} %get-tuple-element.51), channel_id=1, source_target_pairs={{4,0},{8,4},{12,8},{16,12},{20,16},{24,20},{28,24},{0,28},{5,1},{9... | collective-permute-start | bytes 786440 | tf_op jit(solution)/shard_map/ppermute | solution.py:279
  9.2 52.3 %collective-permute-start.12 = (f32[512,128]{1,0:T(8,128)S(1)}, f32[512,128]{1,0:T(8,128)S(1)}, u32[]{:S(2)}, u32[]{:S(2)}) collective-permute-start(f32[512,128]{1,0:T(8,128)S(1)} %get-tuple-element.52), channel_id=1, source_target_pairs={{0,4},{4,8},{8,12},{12,16},{16,20},{20,24},{24,28},{28,0},{1,5},{5... | collective-permute-start | bytes 786440 | tf_op jit(solution)/shard_map/ppermute | solution.py:279
  10.7 43.4 %collective-permute-start = (f32[512,128]{1,0:T(8,128)S(1)}, f32[512,128]{1,0:T(8,128)S(1)}, u32[]{:S(2)}, u32[]{:S(2)}) collective-permute-start(f32[512,128]{1,0:T(8,128)S(1)} %get-tuple-element.53), channel_id=1, source_target_pairs={{0,4},{4,8},{8,12},{12,16},{16,20},{20,24},{24,28},{28,0},{1,5},{5... | collective-permute-start | bytes 786440 | tf_op jit(solution)/shard_map/ppermute | solution.py:279
  17.2 18.8 %copy-start.3 = (f32[4096,256]{1,0:T(8,128)S(1)}, f32[4096,256]{1,0:T(8,128)}, u32[]{:S(2)}) copy-start(f32[4096,256]{1,0:T(8,128)} %v_ref.47) | copy-start | bytes 12582916
  35.3 6.0 %copy-start = (bf16[32,256,768]{2,1,0:T(8,128)(2,1)}, bf16[32,256,768]{2,1,0:T(8,128)(2,1)S(1)}, u32[]{:S(2)}) copy-start(bf16[32,256,768]{2,1,0:T(8,128)(2,1)S(1)} %split_hamiltonian.1.h_ref) | copy-start | bytes 37748740
  42.0 4.6 %copy-start.1 = (bf16[32,256,768]{2,1,0:T(8,128)(2,1)S(1)}, bf16[32,256,768]{2,1,0:T(8,128)(2,1)}, u32[]{:S(2)}) copy-start(bf16[32,256,768]{2,1,0:T(8,128)(2,1)} %copy-done) | copy-start | bytes 37748740
  46.6 2.2 copy-start.4
  56.7 31.6 %collective-permute-start.2 = (f32[512,128]{1,0:T(8,128)S(1)}, f32[512,128]{1,0:T(8,128)S(1)}, u32[]{:S(2)}, u32[]{:S(2)}) collective-permute-start(f32[512,128]{1,0:T(8,128)S(1)} %get-tuple-element.26.rest_4_.rest_2_.rest_7_), channel_id=1, source_target_pairs={{0,4},{4,8},{8,12},{12,16},{16,20},{20,24},{24,28},{28,0},{1,5},{5... | collective-permute-start | bytes 786440 | tf_op jit(solution)/shard_map/ppermute | solution.py:279
  56.8 12.2 %copy-start.5 = (f32[4096,256]{1,0:T(8,128)S(1)}, f32[4096,256]{1,0:T(8,128)}, u32[]{:S(2)}) copy-start(f32[4096,256]{1,0:T(8,128)} %v_ref.47) | copy-start | bytes 12582916
  56.8 31.5 %collective-permute-start.3 = (f32[512,128]{1,0:T(8,128)S(1)}, f32[512,128]{1,0:T(8,128)S(1)}, u32[]{:S(2)}, u32[]{:S(2)}) collective-permute-start(f32[512,128]{1,0:T(8,128)S(1)} %get-tuple-element.27.rest_1_.rest_0_.rest_6_), channel_id=1, source_target_pairs={{4,0},{8,4},{12,8},{16,12},{20,16},{24,20},{28,24},{0,28},{5,1},{9... | collective-permute-start | bytes 786440 | tf_op jit(solution)/shard_map/ppermute | solution.py:279
  64.2 15.2 %collective-permute-start.14 = (f32[512,128]{1,0:T(8,128)S(1)}, f32[512,128]{1,0:T(8,128)S(1)}, u32[]{:S(2)}, u32[]{:S(2)}) collective-permute-start(f32[512,128]{1,0:T(8,128)S(1)} %get-tuple-element.37.rest_4_.rest_2_.rest_7_), channel_id=1, source_target_pairs={{0,4},{4,8},{8,12},{12,16},{16,20},{20,24},{24,28},{28,0},{1,5},{5... | collective-permute-start | bytes 786440 | tf_op jit(solution)/shard_map/ppermute | solution.py:279
  64.2 16.7 %collective-permute-start.15 = (f32[512,128]{1,0:T(8,128)S(1)}, f32[512,128]{1,0:T(8,128)S(1)}, u32[]{:S(2)}, u32[]{:S(2)}) collective-permute-start(f32[512,128]{1,0:T(8,128)S(1)} %get-tuple-element.38.rest_1_.rest_0_.rest_6_), channel_id=1, source_target_pairs={{4,0},{8,4},{12,8},{16,12},{20,16},{24,20},{28,24},{0,28},{5,1},{9... | collective-permute-start | bytes 786440 | tf_op jit(solution)/shard_map/ppermute | solution.py:279
  83.5 32.5 %collective-permute-start.16 = (f32[512,128]{1,0:T(8,128)S(1)}, f32[512,128]{1,0:T(8,128)S(1)}, u32[]{:S(2)}, u32[]{:S(2)}) collective-permute-start(f32[512,128]{1,0:T(8,128)S(1)} %get-tuple-element.39.rest_4_.rest_2_.rest_7_), channel_id=1, source_target_pairs={{0,4},{4,8},{8,12},{12,16},{16,20},{20,24},{24,28},{28,0},{1,5},{5... | collective-permute-start | bytes 786440 | tf_op jit(solution)/shard_map/ppermute | solution.py:279
  83.8 32.2 %collective-permute-start.17 = (f32[512,128]{1,0:T(8,128)S(1)}, f32[512,128]{1,0:T(8,128)S(1)}, u32[]{:S(2)}, u32[]{:S(2)}) collective-permute-start(f32[512,128]{1,0:T(8,128)S(1)} %get-tuple-element.40.rest_1_.rest_0_.rest_6_), channel_id=1, source_target_pairs={{4,0},{8,4},{12,8},{16,12},{20,16},{24,20},{28,24},{0,28},{5,1},{9... | collective-permute-start | bytes 786440 | tf_op jit(solution)/shard_map/ppermute | solution.py:279
  90.9 15.2 %collective-permute-start.4 = (f32[512,128]{1,0:T(8,128)S(1)}, f32[512,128]{1,0:T(8,128)S(1)}, u32[]{:S(2)}, u32[]{:S(2)}) collective-permute-start(f32[512,128]{1,0:T(8,128)S(1)} %get-tuple-element.28.rest_4_.rest_2_.rest_7_), channel_id=1, source_target_pairs={{0,4},{4,8},{8,12},{12,16},{16,20},{20,24},{24,28},{28,0},{1,5},{5... | collective-permute-start | bytes 786440 | tf_op jit(solution)/shard_map/ppermute | solution.py:279
  91.0 17.6 %collective-permute-start.5 = (f32[512,128]{1,0:T(8,128)S(1)}, f32[512,128]{1,0:T(8,128)S(1)}, u32[]{:S(2)}, u32[]{:S(2)}) collective-permute-start(f32[512,128]{1,0:T(8,128)S(1)} %get-tuple-element.29.rest_1_.rest_0_.rest_6_), channel_id=1, source_target_pairs={{4,0},{8,4},{12,8},{16,12},{20,16},{24,20},{28,24},{0,28},{5,1},{9... | collective-permute-start | bytes 786440 | tf_op jit(solution)/shard_map/ppermute | solution.py:279
  111.2 22.6 %collective-permute-start.6 = (f32[512,128]{1,0:T(8,128)S(1)}, f32[512,128]{1,0:T(8,128)S(1)}, u32[]{:S(2)}, u32[]{:S(2)}) collective-permute-start(f32[512,128]{1,0:T(8,128)S(1)} %get-tuple-element.30.rest_4_.rest_2_.rest_7_), channel_id=1, source_target_pairs={{0,4},{4,8},{8,12},{12,16},{16,20},{20,24},{24,28},{28,0},{1,5},{5... | collective-permute-start | bytes 786440 | tf_op jit(solution)/shard_map/ppermute | solution.py:279
  111.2 22.6 %collective-permute-start.7 = (f32[512,128]{1,0:T(8,128)S(1)}, f32[512,128]{1,0:T(8,128)S(1)}, u32[]{:S(2)}, u32[]{:S(2)}) collective-permute-start(f32[512,128]{1,0:T(8,128)S(1)} %get-tuple-element.31.rest_1_.rest_0_.rest_6_), channel_id=1, source_target_pairs={{4,0},{8,4},{12,8},{16,12},{20,16},{24,20},{28,24},{0,28},{5,1},{9... | collective-permute-start | bytes 786440 | tf_op jit(solution)/shard_map/ppermute | solution.py:279
  118.6 22.6 %collective-permute-start.18 = (f32[512,128]{1,0:T(8,128)S(1)}, f32[512,128]{1,0:T(8,128)S(1)}, u32[]{:S(2)}, u32[]{:S(2)}) collective-permute-start(f32[512,128]{1,0:T(8,128)S(1)} %get-tuple-element.41.rest_4_.rest_2_.rest_7_), channel_id=1, source_target_pairs={{0,4},{4,8},{8,12},{12,16},{16,20},{20,24},{24,28},{28,0},{1,5},{5... | collective-permute-start | bytes 786440 | tf_op jit(solution)/shard_map/ppermute | solution.py:279
  118.6 22.6 %collective-permute-start.19 = (f32[512,128]{1,0:T(8,128)S(1)}, f32[512,128]{1,0:T(8,128)S(1)}, u32[]{:S(2)}, u32[]{:S(2)}) collective-permute-start(f32[512,128]{1,0:T(8,128)S(1)} %get-tuple-element.42.rest_1_.rest_0_.rest_6_), channel_id=1, source_target_pairs={{4,0},{8,4},{12,8},{16,12},{20,16},{24,20},{28,24},{0,28},{5,1},{9... | collective-permute-start | bytes 786440 | tf_op jit(solution)/shard_map/ppermute | solution.py:279
  136.4 37.2 %collective-permute-start.8 = (f32[512,128]{1,0:T(8,128)S(1)}, f32[512,128]{1,0:T(8,128)S(1)}, u32[]{:S(2)}, u32[]{:S(2)}) collective-permute-start(f32[512,128]{1,0:T(8,128)S(1)} %get-tuple-element.32.rest_4_.rest_2_.rest_7_), channel_id=1, source_target_pairs={{0,4},{4,8},{8,12},{12,16},{16,20},{20,24},{24,28},{28,0},{1,5},{5... | collective-permute-start | bytes 786440 | tf_op jit(solution)/shard_map/ppermute | solution.py:279
  136.5 37.1 %collective-permute-start.9 = (f32[512,128]{1,0:T(8,128)S(1)}, f32[512,128]{1,0:T(8,128)S(1)}, u32[]{:S(2)}, u32[]{:S(2)}) collective-permute-start(f32[512,128]{1,0:T(8,128)S(1)} %get-tuple-element.33.rest_1_.rest_0_.rest_6_), channel_id=1, source_target_pairs={{4,0},{8,4},{12,8},{16,12},{20,16},{24,20},{28,24},{0,28},{5,1},{9... | collective-permute-start | bytes 786440 | tf_op jit(solution)/shard_map/ppermute | solution.py:279
  143.8 16.9 %collective-permute-start.20 = (f32[512,128]{1,0:T(8,128)S(1)}, f32[512,128]{1,0:T(8,128)S(1)}, u32[]{:S(2)}, u32[]{:S(2)}) collective-permute-start(f32[512,128]{1,0:T(8,128)S(1)} %get-tuple-element.43.rest_4_.rest_2_.rest_7_), channel_id=1, source_target_pairs={{0,4},{4,8},{8,12},{12,16},{16,20},{20,24},{24,28},{28,0},{1,5},{5... | collective-permute-start | bytes 786440 | tf_op jit(solution)/shard_map/ppermute | solution.py:279
  143.9 16.9 %collective-permute-start.21 = (f32[512,128]{1,0:T(8,128)S(1)}, f32[512,128]{1,0:T(8,128)S(1)}, u32[]{:S(2)}, u32[]{:S(2)}) collective-permute-start(f32[512,128]{1,0:T(8,128)S(1)} %get-tuple-element.44.rest_1_.rest_0_.rest_6_), channel_id=1, source_target_pairs={{4,0},{8,4},{12,8},{16,12},{20,16},{24,20},{28,24},{0,28},{5,1},{9... | collective-permute-start | bytes 786440 | tf_op jit(solution)/shard_map/ppermute | solution.py:279
  155.5 20.7 %copy-start.7 = (f32[3072,128]{1,0:T(8,128)}, f32[3072,128]{1,0:T(8,128)S(1)}, u32[]{:S(2)}) copy-start(f32[3072,128]{1,0:T(8,128)S(1)} %interior.16.rest_2_.rest_3_.rest_1_) | copy-start | bytes 4718596
  171.0 1.1 copy-start.9
  172.1 45.6 %collective-permute-start.33 = (f32[1536,128]{1,0:T(8,128)}, f32[1536,128]{1,0:T(8,128)}, u32[]{:S(2)}, u32[]{:S(2)}) collective-permute-start(f32[1536,128]{1,0:T(8,128)} %get-tuple-element.54), channel_id=1, source_target_pairs={{0,2},{1,3},{2,0},{3,1},{4,6},{5,7},{6,4},{7,5},{8,10},{9,11},{10,... | collective-permute-start | bytes 2359304 | tf_op jit(solution)/shard_map/ppermute | solution.py:326
  176.3 8.2 %copy-start.21 = (f32[512,128]{1,0:T(8,128)}, f32[512,128]{1,0:T(8,128)S(1)}, u32[]{:S(2)}) copy-start(f32[512,128]{1,0:T(8,128)S(1)} %get-tuple-element.34.rest_4_.rest_2_) | copy-start | bytes 786436
  176.3 8.2 %copy-start.19 = (f32[512,128]{1,0:T(8,128)}, f32[512,128]{1,0:T(8,128)S(1)}, u32[]{:S(2)}) copy-start(f32[512,128]{1,0:T(8,128)S(1)} %get-tuple-element.35.rest_1_.rest_0_) | copy-start | bytes 786436
  182.7 1.2 copy-start.12
  183.9 33.9 %collective-permute-start.32 = (f32[1536,128]{1,0:T(8,128)}, f32[1536,128]{1,0:T(8,128)}, u32[]{:S(2)}, u32[]{:S(2)}) collective-permute-start(f32[1536,128]{1,0:T(8,128)} %get-tuple-element.56), channel_id=1, source_target_pairs={{0,2},{1,3},{2,0},{3,1},{4,6},{5,7},{6,4},{7,5},{8,10},{9,11},{10,... | collective-permute-start | bytes 2359304 | tf_op jit(solution)/shard_map/ppermute | solution.py:326
  184.4 14.2 %collective-permute-start.10 = (f32[512,128]{1,0:T(8,128)S(1)}, f32[512,128]{1,0:T(8,128)}, u32[]{:S(2)}, u32[]{:S(2)}) collective-permute-start(f32[512,128]{1,0:T(8,128)S(1)} %get-tuple-element.34.rest_4_.rest_2_), channel_id=1, source_target_pairs={{0,4},{4,8},{8,12},{12,16},{16,20},{20,24},{24,28},{28,0},{1,5},{5... | collective-permute-start | bytes 786440 | tf_op jit(solution)/shard_map/ppermute | solution.py:279
  184.4 19.5 %collective-permute-start.11 = (f32[512,128]{1,0:T(8,128)S(1)}, f32[512,128]{1,0:T(8,128)}, u32[]{:S(2)}, u32[]{:S(2)}) collective-permute-start(f32[512,128]{1,0:T(8,128)S(1)} %get-tuple-element.35.rest_1_.rest_0_), channel_id=1, source_target_pairs={{4,0},{8,4},{12,8},{16,12},{20,16},{24,20},{28,24},{0,28},{5,1},{9... | collective-permute-start | bytes 786440 | tf_op jit(solution)/shard_map/ppermute | solution.py:279
  189.1 28.0 %collective-permute-start.22 = (f32[512,128]{1,0:T(8,128)}, f32[512,128]{1,0:T(8,128)}, u32[]{:S(2)}, u32[]{:S(2)}) collective-permute-start(f32[512,128]{1,0:T(8,128)} %get-tuple-element.45.rest_4_.rest_2_), channel_id=1, source_target_pairs={{0,4},{4,8},{8,12},{12,16},{16,20},{20,24},{24,28},{28,0},{1,5},{5... | collective-permute-start | bytes 786440 | tf_op jit(solution)/shard_map/ppermute | solution.py:279
  198.6 20.4 %collective-permute-start.23 = (f32[512,128]{1,0:T(8,128)S(1)}, f32[512,128]{1,0:T(8,128)S(1)}, u32[]{:S(2)}, u32[]{:S(2)}) collective-permute-start(f32[512,128]{1,0:T(8,128)S(1)} %get-tuple-element.46.rest_1_.rest_0_), channel_id=1, source_target_pairs={{4,0},{8,4},{12,8},{16,12},{20,16},{24,20},{28,24},{0,28},{5,1},{9... | collective-permute-start | bytes 786440 | tf_op jit(solution)/shard_map/ppermute | solution.py:279
  203.9 30.9 %collective-permute-start.31 = (f32[1536,128]{1,0:T(8,128)}, f32[1536,128]{1,0:T(8,128)}, u32[]{:S(2)}, u32[]{:S(2)}) collective-permute-start(f32[1536,128]{1,0:T(8,128)} %get-tuple-element.55), channel_id=1, source_target_pairs={{0,1},{1,0},{2,3},{3,2},{4,5},{5,4},{6,7},{7,6},{8,9},{9,8},{10,11... | collective-permute-start | bytes 2359304 | tf_op jit(solution)/shard_map/ppermute | solution.py:326
  203.9 4.6 %copy-start.2 = (bf16[32,256,768]{2,1,0:T(8,128)(2,1)S(1)}, bf16[32,256,768]{2,1,0:T(8,128)(2,1)}, u32[]{:S(2)}) copy-start(bf16[32,256,768]{2,1,0:T(8,128)(2,1)} %copy-done) | copy-start | bytes 37748740
  208.5 2.2 copy-start.6
  210.7 1.4 copy-start.8
  212.1 0.9 copy-start.20
  213.0 0.9 copy-start.22
  217.1 31.0 %copy-start.16 = (f32[512,128]{1,0:T(8,128)}, f32[512,128]{1,0:T(8,128)S(1)}, u32[]{:S(2)}) copy-start(f32[512,128]{1,0:T(8,128)S(1)} %get-tuple-element.48.rest_1_) | copy-start | bytes 786436
  217.2 18.2 %collective-permute-start.30 = (f32[1536,128]{1,0:T(8,128)}, f32[1536,128]{1,0:T(8,128)}, u32[]{:S(2)}, u32[]{:S(2)}) collective-permute-start(f32[1536,128]{1,0:T(8,128)} %get-tuple-element.57), channel_id=1, source_target_pairs={{0,1},{1,0},{2,3},{3,2},{4,5},{5,4},{6,7},{7,6},{8,9},{9,8},{10,11... | collective-permute-start | bytes 2359304 | tf_op jit(solution)/shard_map/ppermute | solution.py:326
  217.7 17.7 %collective-permute-start.35 = (f32[1536,128]{1,0:T(8,128)}, f32[1536,128]{1,0:T(8,128)}, u32[]{:S(2)}, u32[]{:S(2)}) collective-permute-start(f32[1536,128]{1,0:T(8,128)} %collective-permute-done.33.rest_5_), channel_id=1, source_target_pairs={{0,1},{1,0},{2,3},{3,2},{4,5},{5,4},{6,7},{7,6},{8,9},{9,8},{10,11... | collective-permute-start | bytes 2359304 | tf_op jit(solution)/shard_map/ppermute | solution.py:326
  217.8 18.1 %collective-permute-start.34 = (f32[1536,128]{1,0:T(8,128)}, f32[1536,128]{1,0:T(8,128)}, u32[]{:S(2)}, u32[]{:S(2)}) collective-permute-start(f32[1536,128]{1,0:T(8,128)} %collective-permute-done.32.rest_4_), channel_id=1, source_target_pairs={{0,1},{1,0},{2,3},{3,2},{4,5},{5,4},{6,7},{7,6},{8,9},{9,8},{10,11... | collective-permute-start | bytes 2359304 | tf_op jit(solution)/shard_map/ppermute | solution.py:326
  219.0 8.4 %collective-permute-start.26 = (f32[512,128]{1,0:T(8,128)S(1)}, f32[512,128]{1,0:T(8,128)}, u32[]{:S(2)}, u32[]{:S(2)}) collective-permute-start(f32[512,128]{1,0:T(8,128)S(1)} %get-tuple-element.62), channel_id=1, source_target_pairs={{0,2},{1,3},{2,0},{3,1},{4,6},{5,7},{6,4},{7,5},{8,10},{9,11},{10,... | collective-permute-start | bytes 786440 | tf_op jit(solution)/shard_map/ppermute | solution.py:326
  223.7 24.5 %copy-start.17 = (f32[512,128]{1,0:T(8,128)}, f32[512,128]{1,0:T(8,128)S(1)}, u32[]{:S(2)}) copy-start(f32[512,128]{1,0:T(8,128)S(1)} %get-tuple-element.47.rest_2_) | copy-start | bytes 786436
  223.7 24.5 %copy-start.18 = (f32[512,128]{1,0:T(8,128)}, f32[512,128]{1,0:T(8,128)S(1)}, u32[]{:S(2)}) copy-start(f32[512,128]{1,0:T(8,128)S(1)} %get-tuple-element.49.rest_3_) | copy-start | bytes 786436
  227.4 7.5 %collective-permute-start.27 = (f32[512,128]{1,0:T(8,128)S(1)}, f32[512,128]{1,0:T(8,128)S(1)}, u32[]{:S(2)}, u32[]{:S(2)}) collective-permute-start(f32[512,128]{1,0:T(8,128)S(1)} %get-tuple-element.60), channel_id=1, source_target_pairs={{0,2},{1,3},{2,0},{3,1},{4,6},{5,7},{6,4},{7,5},{8,10},{9,11},{10,... | collective-permute-start | bytes 786440 | tf_op jit(solution)/shard_map/ppermute | solution.py:326
  234.8 13.2 %collective-permute-start.24 = (f32[512,128]{1,0:T(8,128)}, f32[512,128]{1,0:T(8,128)S(1)}, u32[]{:S(2)}, u32[]{:S(2)}) collective-permute-start(f32[512,128]{1,0:T(8,128)} %get-tuple-element.63), channel_id=1, source_target_pairs={{0,1},{1,0},{2,3},{3,2},{4,5},{5,4},{6,7},{7,6},{8,9},{9,8},{10,11... | collective-permute-start | bytes 786440 | tf_op jit(solution)/shard_map/ppermute | solution.py:326
  234.9 13.3 %collective-permute-start.25 = (f32[512,128]{1,0:T(8,128)S(1)}, f32[512,128]{1,0:T(8,128)S(1)}, u32[]{:S(2)}, u32[]{:S(2)}) collective-permute-start(f32[512,128]{1,0:T(8,128)S(1)} %get-tuple-element.61), channel_id=1, source_target_pairs={{0,1},{1,0},{2,3},{3,2},{4,5},{5,4},{6,7},{7,6},{8,9},{9,8},{10,11... | collective-permute-start | bytes 786440 | tf_op jit(solution)/shard_map/ppermute | solution.py:326
  235.4 12.8 %collective-permute-start.28 = (f32[512,128]{1,0:T(8,128)}, f32[512,128]{1,0:T(8,128)S(1)}, u32[]{:S(2)}, u32[]{:S(2)}) collective-permute-start(f32[512,128]{1,0:T(8,128)} %collective-permute-done.26.rest_6_), channel_id=1, source_target_pairs={{0,1},{1,0},{2,3},{3,2},{4,5},{5,4},{6,7},{7,6},{8,9},{9,8},{10,11... | collective-permute-start | bytes 786440 | tf_op jit(solution)/shard_map/ppermute | solution.py:326
  235.4 12.7 %collective-permute-start.29 = (f32[512,128]{1,0:T(8,128)S(1)}, f32[512,128]{1,0:T(8,128)S(1)}, u32[]{:S(2)}, u32[]{:S(2)}) collective-permute-start(f32[512,128]{1,0:T(8,128)S(1)} %collective-permute-done.27.rest_7_), channel_id=1, source_target_pairs={{0,1},{1,0},{2,3},{3,2},{4,5},{5,4},{6,7},{7,6},{8,9},{9,8},{10,11... | collective-permute-start | bytes 786440 | tf_op jit(solution)/shard_map/ppermute | solution.py:326
  235.9 1.4 copy-start.10
  237.3 1.4 copy-start.13
  251.9 1.0 copy-start.15
  252.9 46.7 %copy-start.11 = (f32[3072,128]{1,0:T(8,128)S(1)}, f32[3072,128]{1,0:T(8,128)}, u32[]{:S(2)}) copy-start(f32[3072,128]{1,0:T(8,128)} %copy-done.9) | copy-start | bytes 4718596
  252.9 46.7 %copy-start.14 = (f32[3072,128]{1,0:T(8,128)S(1)}, f32[3072,128]{1,0:T(8,128)}, u32[]{:S(2)}) copy-start(f32[3072,128]{1,0:T(8,128)} %copy-done.12) | copy-start | bytes 4718596
  259.3 13.9 %collective-permute-start.36 = (f32[4,256,128]{2,1,0:T(8,128)}, f32[4,256,128]{2,1,0:T(8,128)}, u32[]{:S(2)}, u32[]{:S(2)}) collective-permute-start(f32[4,256,128]{2,1,0:T(8,128)} %bitcast.3), channel_id=1, source_target_pairs={{0,4},{4,0},{8,12},{12,8},{16,20},{20,16},{24,28},{28,24},{1,5},{5... | collective-permute-start | bytes 1572872 | tf_op jit(solution)/shard_map/ppermute | solution.py:359
  276.0 7.4 %collective-permute-start.37 = (f32[2,256,128]{2,1,0:T(8,128)}, f32[2,256,128]{2,1,0:T(8,128)}, u32[]{:S(2)}, u32[]{:S(2)}) collective-permute-start(f32[2,256,128]{2,1,0:T(8,128)} %dynamic-slice_bitcast_fusion), channel_id=1, source_target_pairs={{0,8},{4,12},{8,0},{12,4},{16,24},{20,28},{24,16},{28,20},{1,9},{5... | collective-permute-start | bytes 786440 | tf_op jit(solution)/shard_map/ppermute | solution.py:359
  285.2 7.4 %collective-permute-start.38 = (f32[1,256,128]{2,1,0:T(8,128)S(1)}, f32[1,256,128]{2,1,0:T(8,128)}, u32[]{:S(2)}, u32[]{:S(2)}) collective-permute-start(f32[1,256,128]{2,1,0:T(8,128)S(1)} %constant_dynamic-slice_fusion.2), channel_id=1, source_target_pairs={{0,16},{4,20},{8,24},{12,28},{16,0},{20,4},{24,8},{28,12},{1,17},{... | collective-permute-start | bytes 393224 | tf_op jit(solution)/shard_map/ppermute | solution.py:359
  297.4 5.8 %collective-permute-start.39 = (f32[128,128]{0,1:T(8,128)}, f32[128,128]{0,1:T(8,128)S(1)}, u32[]{:S(2)}, u32[]{:S(2)}) collective-permute-start(f32[128,128]{0,1:T(8,128)} %bitcast.27), channel_id=1, source_target_pairs={{0,0},{1,8},{2,16},{3,24},{4,4},{5,12},{6,20},{7,28},{8,1},{9,9},{... | collective-permute-start | bytes 196616 | tf_op jit(solution)/shard_map/ppermute | solution.py:371
  298.9 4.5 %collective-permute-start.40 = (f32[128,128]{0,1:T(8,128)}, f32[128,128]{0,1:T(8,128)S(1)}, u32[]{:S(2)}, u32[]{:S(2)}) collective-permute-start(f32[128,128]{0,1:T(8,128)} %bitcast.26), channel_id=1, source_target_pairs={{0,4},{1,12},{2,20},{3,28},{4,0},{5,8},{6,16},{7,24},{8,5},{9,13},... | collective-permute-start | bytes 196616 | tf_op jit(solution)/shard_map/ppermute | solution.py:371
  (2 other events, 1.5 us)
